TPU v7x, 512 devices: a whole 4x4x16 slice. The times are simulated.
512 devices in a mesh: row: 2 (over y_hi), grp: 4 (over x), sec: 64 (over z, y_lo, core).
Axes of the slice: x: 4, y: 4 (y_hi: 2, y_lo: 2; y = y_hi * 2 + y_lo), z: 16, core: 2. Of those that a mesh axis runs over, the one named last changes fastest.
Arguments:
- state: float32 [2, 5, 1024, 8192], P('row', None, 'grp', 'sec'), may hold values from -6 to 6
- damping: float32 [2, 1024, 8192], P('row', 'grp', 'sec'), may hold values from 0.1 to 1
- jac_axial: float32 [2, 5, 5], P('row'), may hold values from -2.5 to 2.5
- jac_angular: float32 [2, 5, 5], P('row'), may hold values from -2.5 to 2.5
- section_shift: int32 [3], replicated, may hold values from 0 to 63, as said below
- donor_offset: int32 [8192], replicated, may hold values from 0 to 3
- match_weight: float32 [4, 8192], replicated, may hold values from 0.1 to 1
Outputs:
- advanced: float32 [2, 5, 1024, 8192], P('row', None, 'grp', 'sec')
Inputs may be any that keep to these rules, and one draw needn't show every extreme that they name: `section_shift`: whole-sector rotation of the rotor against the stator at each section; one section shifts by 32 sectors and another by 64 - 1.
All inputs are finite; a program needn't handle non-finite values.
Results may differ from a plain program's by a relative error of at most 0.00002.
Values sent between devices are 32-bit elements; how exact they have to be, the bound alone decides.
No kernel may reach another device: no remote copies, remote signals or barrier semaphores. Data moves between devices by JAX's collectives and lax.ppermute only.
A program may use at most 64 MiB of HBM per device.

v0:
```python
import jax
import jax.numpy as jnp
from jax import lax
from jax.sharding import PartitionSpec as P

DONORS = 4


time_step = 0.3
viscosity = 0.05
lead_width = 8


def partner_2(x, axis, bit):
    return lax.ppermute(x, axis, [(i, i ^ 1 << bit) for i in range(lax.axis_size(axis))])


def extended_2(block, sides, width, periodic):
    for axis, dim in sides:
        count = lax.axis_size(axis)
        forward = [(i, i + 1) for i in range(count - 1)]
        if periodic:
            forward.append((count - 1, 0))
        backward = [(target, source) for source, target in forward]
        low = lax.ppermute(
            lax.slice_in_dim(block, block.shape[dim] - width, None, axis=dim), axis, forward
        )
        high = lax.ppermute(lax.slice_in_dim(block, 0, width, axis=dim), axis, backward)
        block = jnp.concatenate([low, block, high], axis=dim)
    return block


def stencil(padded, axis, count):

    def window(offset):
        return lax.slice_in_dim(padded, 2 + offset, 2 + offset + count, axis=axis)

    first = (8.0 * (window(1) - window(-1)) - (window(2) - window(-2))) / 12.0
    second = window(1) - 2.0 * window(0) + window(-1)
    return (first, second)


def apply_matrix(matrix, fields):
    results = []
    for target in range(5):
        total = matrix[target, 0] * fields[0]
        for source in range(1, 5):
            total = total + matrix[target, source] * fields[source]
        results.append(total)
    return jnp.stack(results)


def tendency(fields, q_padded, t_padded, axial, angular, damping):
    grad_q, lap_q = stencil(q_padded, 1, fields.shape[1])
    grad_t, lap_t = stencil(t_padded, 2, fields.shape[2])
    flux = apply_matrix(axial, grad_q) + apply_matrix(angular, grad_t)
    return viscosity * (lap_q + lap_t) - flux - damping * fields


def shards(state, damping, jac_axial, jac_angular, section_shift, donor_offset, match_weight):
    coeff = damping[0]
    axial = 0.5 * (jac_axial + jnp.swapaxes(jac_axial, 1, 2))[0]
    angular = 0.5 * (jac_angular + jnp.swapaxes(jac_angular, 1, 2))[0]
    depth = state.shape[2]
    width = state.shape[3]
    groups = lax.axis_size("grp")
    sectors = lax.axis_size("sec")
    at_interface = lax.axis_index("grp") == groups - 1
    sector = lax.axis_index("sec")
    direction_sign = 1 - 2 * lax.axis_index("row")
    weights = match_weight / jnp.sum(match_weight, axis=0)
    local_weights = lax.dynamic_slice_in_dim(weights, sector * width, width, 1)
    local_offset = lax.dynamic_slice_in_dim(donor_offset, sector * width, width, 0)
    local_angle = jnp.arange(width, dtype=jnp.int32)

    def interface(fields, shift):
        layers = jnp.stack([fields[:, depth - 1, :], fields[:, depth - 2, :]], axis=1)
        partner = partner_2(layers, "row", 0)
        amount = direction_sign * shift % sectors
        collected = lax.all_gather(partner, "sec", axis=2, tiled=True)
        extended = jnp.concatenate([collected, collected[:, :, :lead_width]], axis=2)
        start = (sector + amount) % sectors * width
        window = lax.dynamic_slice_in_dim(extended, start, width + lead_width, 2)
        total = jnp.zeros(partner.shape, jnp.float32)
        for donor in range(DONORS):
            index = local_angle + local_offset + donor
            total = total + local_weights[donor] * jnp.take(window, index, axis=2)
        return total

    def rhs(current, shift):
        fields = current[0]
        edge = interface(fields, shift)
        padded_q = extended_2(fields, (("grp", 1),), 2, False)
        upper = jnp.where(at_interface, edge, padded_q[:, depth + 2 :, :])
        q_padded = jnp.concatenate([padded_q[:, : depth + 2, :], upper], axis=1)
        t_padded = extended_2(fields, (("sec", 2),), 2, True)
        return tendency(fields, q_padded, t_padded, axial, angular, coeff)[None]

    first = state + time_step * rhs(state, section_shift[0])
    second = 0.75 * state + 0.25 * (first + time_step * rhs(first, section_shift[1]))
    return state / 3.0 + 2.0 / 3.0 * (second + time_step * rhs(second, section_shift[2]))


def solution(mesh):
    return jax.shard_map(
        shards,
        mesh=mesh,
        in_specs=(
            P("row", None, "grp", "sec"),
            P("row", "grp", "sec"),
            P("row", None, None),
            P("row", None, None),
            P(),
            P(),
            P(),
        ),
        out_specs=P("row", None, "grp", "sec"),
        check_vma=False,
    )
```

profile of v0, /device:TPU:6, one launch (start us, length us, event | category | flops | bytes accessed | tf_op | source)
XLA Modules:
  0.0 366.9 jit_solution(3431298533968664160)
XLA Ops:
  5.7 5.1 %collective-permute-start = (f32[5,2,128]{2,1,0:T(2,128)S(1)}, f32[5,2,128]{2,1,0:T(2,128)S(1)}, u32[]{:S(2)}, u32[]{:S(2)}) collective-permute-start(f32[5,2,128]{2,1,0:T(2,128)S(1)} %pad_maximum_fusion.12), channel_id=1, source_target_pairs={{0,256},{256,0},{1,257},{257,1},{2,258},{258,2},{3,259},{259,3},{4... | collective-permute-start | bytes 15368 | tf_op jit(solution)/shard_map/ppermute | solution.py:15
  14.7 10.4 %collective-permute-start.3 = (f32[5,256,2]{1,2,0:T(2,128)S(1)}, f32[5,256,2]{1,2,0:T(2,128)S(1)}, u32[]{:S(2)}, u32[]{:S(2)}) collective-permute-start(f32[5,256,2]{1,2,0:T(2,128)S(1)} %copy.362), channel_id=1, source_target_pairs={{1,0},{2,1},{3,2},{4,3},{5,4},{6,5},{7,6},{8,7},{9,8},{10,9},{11,1... | collective-permute-start | bytes 30728 | tf_op jit(solution)/shard_map/ppermute | solution.py:28
  31.7 63.0 %all_gather.9 = f32[5,2,8192]{2,1,0:T(2,128)S(1)} all-gather(f32[5,2,128]{2,1,0:T(2,128)S(1)} %collective-permute-done), channel_id=1, replica_groups=mesh['row'=2,'grp'=4,'sec'=64] {'sec'}, dimensions={2}, use_global_device_ids=true | all-gather | bytes 332800 | tf_op jit(solution)/shard_map/all_gather | solution.py:80
  100.9 3.2 add_dynamic-update-slice_fusion.24
  104.1 3.2 add_dynamic-update-slice_fusion.23
  110.5 3.2 add_dynamic-update-slice_fusion.21
  123.1 3.2 add_dynamic-update-slice_fusion.27
  133.7 3.7 %collective-permute-start.5 = (f32[5,2,128]{2,1,0:T(2,128)S(1)}, f32[5,2,128]{2,1,0:T(2,128)S(1)}, u32[]{:S(2)}, u32[]{:S(2)}) collective-permute-start(f32[5,2,128]{2,1,0:T(2,128)S(1)} %pad_maximum_fusion.13), channel_id=1, source_target_pairs={{0,256},{256,0},{1,257},{257,1},{2,258},{258,2},{3,259},{259,3},{4... | collective-permute-start | bytes 15368 | tf_op jit(solution)/shard_map/ppermute | solution.py:15
  137.4 4.5 %collective-permute-start.6 = (f32[5,2,128]{2,1,0:T(2,128)S(1)}, f32[5,2,128]{2,1,0:T(2,128)S(1)}, u32[]{:S(2)}, u32[]{:S(2)}) collective-permute-start(f32[5,2,128]{2,1,0:T(2,128)S(1)} %get-tuple-element.28), channel_id=1, source_target_pairs={{64,0},{128,64},{192,128},{65,1},{129,65},{193,129},{66,2},{130,66... | collective-permute-start | bytes 15368 | tf_op jit(solution)/shard_map/ppermute | solution.py:28
  145.7 5.8 %collective-permute-start.8 = (f32[5,256,2]{1,2,0:T(2,128)S(1)}, f32[5,256,2]{1,2,0:T(2,128)S(1)}, u32[]{:S(2)}, u32[]{:S(2)}) collective-permute-start(f32[5,256,2]{1,2,0:T(2,128)S(1)} %copy.375), channel_id=1, source_target_pairs={{1,0},{2,1},{3,2},{4,3},{5,4},{6,5},{7,6},{8,7},{9,8},{10,9},{11,1... | collective-permute-start | bytes 30728 | tf_op jit(solution)/shard_map/ppermute | solution.py:28
  151.4 60.3 %all_gather.10 = f32[5,2,8192]{2,1,0:T(2,128)S(1)} all-gather(f32[5,2,128]{2,1,0:T(2,128)S(1)} %collective-permute-done.5), channel_id=1, replica_groups=mesh['row'=2,'grp'=4,'sec'=64] {'sec'}, dimensions={2}, use_global_device_ids=true | all-gather | bytes 332800 | tf_op jit(solution)/shard_map/all_gather | solution.py:80
  217.5 3.2 add_dynamic-update-slice_fusion.14
  220.7 3.2 add_dynamic-update-slice_fusion.13
  227.0 3.2 add_dynamic-update-slice_fusion.11
  233.4 3.2 add_dynamic-update-slice_fusion.19
  239.7 3.2 add_dynamic-update-slice_fusion.17
  250.2 3.6 collective-permute-start.10
  253.8 4.5 %collective-permute-start.11 = (f32[5,2,128]{2,1,0:T(2,128)S(1)}, f32[5,2,128]{2,1,0:T(2,128)S(1)}, u32[]{:S(2)}, u32[]{:S(2)}) collective-permute-start(f32[5,2,128]{2,1,0:T(2,128)S(1)} %get-tuple-element.20), channel_id=1, source_target_pairs={{64,0},{128,64},{192,128},{65,1},{129,65},{193,129},{66,2},{130,66... | collective-permute-start | bytes 15368 | tf_op jit(solution)/shard_map/ppermute | solution.py:28
  262.0 5.8 %collective-permute-start.13 = (f32[5,256,2]{1,2,0:T(2,128)S(1)}, f32[5,256,2]{1,2,0:T(2,128)S(1)}, u32[]{:S(2)}, u32[]{:S(2)}) collective-permute-start(f32[5,256,2]{1,2,0:T(2,128)S(1)} %copy.384), channel_id=1, source_target_pairs={{1,0},{2,1},{3,2},{4,3},{5,4},{6,5},{7,6},{8,7},{9,8},{10,9},{11,1... | collective-permute-start | bytes 30728 | tf_op jit(solution)/shard_map/ppermute | solution.py:28
  267.8 60.2 %all_gather.11 = f32[5,2,8192]{2,1,0:T(2,128)S(1)} all-gather(f32[5,2,128]{2,1,0:T(2,128)S(1)} %collective-permute-done.10), channel_id=1, replica_groups=mesh['row'=2,'grp'=4,'sec'=64] {'sec'}, dimensions={2}, use_global_device_ids=true | all-gather | bytes 332800 | tf_op jit(solution)/shard_map/all_gather | solution.py:80
  333.7 3.2 add_dynamic-update-slice_fusion.4
  336.9 3.2 add_dynamic-update-slice_fusion.3
  343.2 3.2 add_dynamic-update-slice_fusion.1
  355.9 3.2 add_dynamic-update-slice_fusion.7
  (135 shorter events, 95.4 us)
Async XLA Ops:
  0.8 97.6 %collective-permute-start.1 = (f32[5,2,128]{2,1,0:T(2,128)S(1)}, f32[5,2,128]{2,1,0:T(2,128)S(1)}, u32[]{:S(2)}, u32[]{:S(2)}) collective-permute-start(f32[5,2,128]{2,1,0:T(2,128)S(1)} %get-tuple-element.36), channel_id=1, source_target_pairs={{64,0},{128,64},{192,128},{65,1},{129,65},{193,129},{66,2},{130,66... | collective-permute-start | bytes 15368 | tf_op jit(solution)/shard_map/ppermute | solution.py:28
  3.5 95.5 %collective-permute-start.2 = (f32[5,2,128]{2,1,0:T(2,128)S(1)}, f32[5,2,128]{2,1,0:T(2,128)S(1)}, u32[]{:S(2)}, u32[]{:S(2)}) collective-permute-start(f32[5,2,128]{2,1,0:T(2,128)S(1)} %get-tuple-element.37), channel_id=1, source_target_pairs={{0,64},{64,128},{128,192},{1,65},{65,129},{129,193},{2,66},{66,130... | collective-permute-start | bytes 15368 | tf_op jit(solution)/shard_map/ppermute | solution.py:25
  5.7 26.1 %collective-permute-start = (f32[5,2,128]{2,1,0:T(2,128)S(1)}, f32[5,2,128]{2,1,0:T(2,128)S(1)}, u32[]{:S(2)}, u32[]{:S(2)}) collective-permute-start(f32[5,2,128]{2,1,0:T(2,128)S(1)} %pad_maximum_fusion.12), channel_id=1, source_target_pairs={{0,256},{256,0},{1,257},{257,1},{2,258},{258,2},{3,259},{259,3},{4... | collective-permute-start | bytes 15368 | tf_op jit(solution)/shard_map/ppermute | solution.py:15
  12.3 13.6 %copy-start.3 = (f32[1,5,5]{2,0,1:T(1,128)S(1)}, f32[1,5,5]{2,0,1:T(1,128)}, u32[]{:S(2)}) copy-start(f32[1,5,5]{2,0,1:T(1,128)} %param.12) | copy-start | bytes 304
  12.3 15.1 %copy-start.4 = (f32[1,5,5]{2,0,1:T(1,128)S(1)}, f32[1,5,5]{2,0,1:T(1,128)}, u32[]{:S(2)}) copy-start(f32[1,5,5]{2,0,1:T(1,128)} %param.11) | copy-start | bytes 304
  12.3 16.6 %copy-start.5 = (s32[3]{0:T(128)S(1)}, s32[3]{0:T(128)}, u32[]{:S(2)}) copy-start(s32[3]{0:T(128)} %param.13) | copy-start | bytes 40
  12.3 17.2 %copy-start.2 = (f32[4,8192]{1,0:T(4,128)S(1)}, f32[4,8192]{1,0:T(4,128)}, u32[]{:S(2)}) copy-start(f32[4,8192]{1,0:T(4,128)} %param.15) | copy-start | bytes 393220
  12.6 86.1 %collective-permute-start.4 = (f32[5,256,2]{1,2,0:T(2,128)S(1)}, f32[5,256,2]{1,2,0:T(2,128)S(1)}, u32[]{:S(2)}, u32[]{:S(2)}) collective-permute-start(f32[5,256,2]{1,2,0:T(2,128)S(1)} %copy.364), channel_id=1, source_target_pairs={{0,1},{1,2},{2,3},{3,4},{4,5},{5,6},{6,7},{7,8},{8,9},{9,10},{10,1... | collective-permute-start | bytes 30728 | tf_op jit(solution)/shard_map/ppermute | solution.py:25
  14.7 83.7 %collective-permute-start.3 = (f32[5,256,2]{1,2,0:T(2,128)S(1)}, f32[5,256,2]{1,2,0:T(2,128)S(1)}, u32[]{:S(2)}, u32[]{:S(2)}) collective-permute-start(f32[5,256,2]{1,2,0:T(2,128)S(1)} %copy.362), channel_id=1, source_target_pairs={{1,0},{2,1},{3,2},{4,3},{5,4},{6,5},{7,6},{8,7},{9,8},{10,9},{11,1... | collective-permute-start | bytes 30728 | tf_op jit(solution)/shard_map/ppermute | solution.py:28
  98.4 1.1 copy-start
  126.3 6.2 %copy-start.1 = (f32[1,256,128]{2,1,0:T(8,128)S(1)}, f32[1,256,128]{2,1,0:T(8,128)}, u32[]{:S(2)}) copy-start(f32[1,256,128]{2,1,0:T(8,128)} %param.10) | copy-start | bytes 393220
  133.7 17.8 %collective-permute-start.5 = (f32[5,2,128]{2,1,0:T(2,128)S(1)}, f32[5,2,128]{2,1,0:T(2,128)S(1)}, u32[]{:S(2)}, u32[]{:S(2)}) collective-permute-start(f32[5,2,128]{2,1,0:T(2,128)S(1)} %pad_maximum_fusion.13), channel_id=1, source_target_pairs={{0,256},{256,0},{1,257},{257,1},{2,258},{258,2},{3,259},{259,3},{4... | collective-permute-start | bytes 15368 | tf_op jit(solution)/shard_map/ppermute | solution.py:15
  137.4 78.0 %collective-permute-start.6 = (f32[5,2,128]{2,1,0:T(2,128)S(1)}, f32[5,2,128]{2,1,0:T(2,128)S(1)}, u32[]{:S(2)}, u32[]{:S(2)}) collective-permute-start(f32[5,2,128]{2,1,0:T(2,128)S(1)} %get-tuple-element.28), channel_id=1, source_target_pairs={{64,0},{128,64},{192,128},{65,1},{129,65},{193,129},{66,2},{130,66... | collective-permute-start | bytes 15368 | tf_op jit(solution)/shard_map/ppermute | solution.py:28
  142.0 74.0 %collective-permute-start.7 = (f32[5,2,128]{2,1,0:T(2,128)S(1)}, f32[5,2,128]{2,1,0:T(2,128)S(1)}, u32[]{:S(2)}, u32[]{:S(2)}) collective-permute-start(f32[5,2,128]{2,1,0:T(2,128)S(1)} %get-tuple-element.29), channel_id=1, source_target_pairs={{0,64},{64,128},{128,192},{1,65},{65,129},{129,193},{2,66},{66,130... | collective-permute-start | bytes 15368 | tf_op jit(solution)/shard_map/ppermute | solution.py:25
  143.7 72.0 %collective-permute-start.9 = (f32[5,256,2]{1,2,0:T(2,128)S(1)}, f32[5,256,2]{1,2,0:T(2,128)S(1)}, u32[]{:S(2)}, u32[]{:S(2)}) collective-permute-start(f32[5,256,2]{1,2,0:T(2,128)S(1)} %copy.377), channel_id=1, source_target_pairs={{0,1},{1,2},{2,3},{3,4},{4,5},{5,6},{6,7},{7,8},{8,9},{9,10},{10,1... | collective-permute-start | bytes 30728 | tf_op jit(solution)/shard_map/ppermute | solution.py:25
  145.7 69.8 %collective-permute-start.8 = (f32[5,256,2]{1,2,0:T(2,128)S(1)}, f32[5,256,2]{1,2,0:T(2,128)S(1)}, u32[]{:S(2)}, u32[]{:S(2)}) collective-permute-start(f32[5,256,2]{1,2,0:T(2,128)S(1)} %copy.375), channel_id=1, source_target_pairs={{1,0},{2,1},{3,2},{4,3},{5,4},{6,5},{7,6},{8,7},{9,8},{10,9},{11,1... | collective-permute-start | bytes 30728 | tf_op jit(solution)/shard_map/ppermute | solution.py:28
  250.2 17.6 %collective-permute-start.10 = (f32[5,2,128]{2,1,0:T(2,128)S(1)}, f32[5,2,128]{2,1,0:T(2,128)S(1)}, u32[]{:S(2)}, u32[]{:S(2)}) collective-permute-start(f32[5,2,128]{2,1,0:T(2,128)S(1)} %pad_maximum_fusion.14), channel_id=1, source_target_pairs={{0,256},{256,0},{1,257},{257,1},{2,258},{258,2},{3,259},{259,3},{4... | collective-permute-start | bytes 15368 | tf_op jit(solution)/shard_map/ppermute | solution.py:15
  253.8 77.8 %collective-permute-start.11 = (f32[5,2,128]{2,1,0:T(2,128)S(1)}, f32[5,2,128]{2,1,0:T(2,128)S(1)}, u32[]{:S(2)}, u32[]{:S(2)}) collective-permute-start(f32[5,2,128]{2,1,0:T(2,128)S(1)} %get-tuple-element.20), channel_id=1, source_target_pairs={{64,0},{128,64},{192,128},{65,1},{129,65},{193,129},{66,2},{130,66... | collective-permute-start | bytes 15368 | tf_op jit(solution)/shard_map/ppermute | solution.py:28
  258.4 73.8 %collective-permute-start.12 = (f32[5,2,128]{2,1,0:T(2,128)S(1)}, f32[5,2,128]{2,1,0:T(2,128)S(1)}, u32[]{:S(2)}, u32[]{:S(2)}) collective-permute-start(f32[5,2,128]{2,1,0:T(2,128)S(1)} %get-tuple-element.21), channel_id=1, source_target_pairs={{0,64},{64,128},{128,192},{1,65},{65,129},{129,193},{2,66},{66,130... | collective-permute-start | bytes 15368 | tf_op jit(solution)/shard_map/ppermute | solution.py:25
  260.1 71.8 %collective-permute-start.14 = (f32[5,256,2]{1,2,0:T(2,128)S(1)}, f32[5,256,2]{1,2,0:T(2,128)S(1)}, u32[]{:S(2)}, u32[]{:S(2)}) collective-permute-start(f32[5,256,2]{1,2,0:T(2,128)S(1)} %copy.386), channel_id=1, source_target_pairs={{0,1},{1,2},{2,3},{3,4},{4,5},{5,6},{6,7},{7,8},{8,9},{9,10},{10,1... | collective-permute-start | bytes 30728 | tf_op jit(solution)/shard_map/ppermute | solution.py:25
  262.0 69.6 %collective-permute-start.13 = (f32[5,256,2]{1,2,0:T(2,128)S(1)}, f32[5,256,2]{1,2,0:T(2,128)S(1)}, u32[]{:S(2)}, u32[]{:S(2)}) collective-permute-start(f32[5,256,2]{1,2,0:T(2,128)S(1)} %copy.384), channel_id=1, source_target_pairs={{1,0},{2,1},{3,2},{4,3},{5,4},{6,5},{7,6},{8,7},{9,8},{10,9},{11,1... | collective-permute-start | bytes 30728 | tf_op jit(solution)/shard_map/ppermute | solution.py:28
where the time goes:
time: 372 us; the launch traced here: 367 us
  blocking collectives  183 us (49%)
  other arithmetic  103 us (28%)
  starting transfers between devices  55.8 us (15%)
  local copies, waits for them, and re-layouts  21.2 us (6%)
    all_gather x3, blocking collectives, interface(): collected = lax.all_gather(partner, 'sec', axis=2, tiled=True)  183 us
    unnamed x24, other arithmetic  76.2 us
    ppermute x6, starting transfers between devices, extended_2(): lax.ppermute(lax.slice_in_dim(block, 0, width, axis=dim), axis, backward)  33.7 us
    another operation x6, other arithmetic, apply_matrix(): return jnp.stack(results)  18.3 us
    ppermute x3, starting transfers between devices, partner_2(): lax.ppermute(x, axis, [(i, i ^ 1 << bit) for i in range(lax.axis_size(axi...  12.4 us
    gather x24, local copies, waits for them, and re-layouts, interface(): total = total + local_weights[donor] * jnp.take(window, index, axis=2)  10 us
    ppermute x6, starting transfers between devices, extended_2(): lax.ppermute(lax.slice_in_dim(block, block.shape[dim] - width, None, axis...  9.64 us
  transfers between devices with their start and end apart: 15, of which 0 were waited for; matrix products, arithmetic and copies ran while one was open for 6% of the time, Pallas kernels for 0%

commit v1 on v0

v1 whole, which is shorter than its diff:
```python
import functools

import jax
import jax.numpy as jnp
from jax import lax
from jax.experimental import pallas as pl
from jax.experimental.pallas import tpu as pltpu
from jax.sharding import PartitionSpec as P

DONORS = 4
FIELDS = 5
STEP = 0.3
VISCOSITY = 0.05
AXES = ("row", "grp", "sec")

EDGE = 8
WIDE = 24
PACK = 16
REACH = 6

VMEM = pl.BlockSpec(memory_space=pltpu.VMEM)
SMEM = pl.BlockSpec(memory_space=pltpu.SMEM)


def lanes(shape):
    return lax.broadcasted_iota(jnp.int32, shape, len(shape) - 1)


def scaled_matrices(axial_ref, angular_ref):
    scale = STEP * 2.0 / 3.0 * 0.5

    def one(ref):
        rows = [[None] * FIELDS for _ in range(FIELDS)]
        for i in range(FIELDS):
            for j in range(i, FIELDS):
                rows[i][j] = rows[j][i] = scale * (ref[0, i, j] + ref[0, j, i])
        return rows

    return one(axial_ref), one(angular_ref)


def increments(load, damping, matrices, width):
    axial, angular = matrices
    centre, grad_q, grad_t, lap = [], [], [], []
    for f in range(FIELDS):
        x = load(f, 0)
        down1, up1 = load(f, -1)[:, :width], load(f, 1)[:, :width]
        down2, up2 = load(f, -2)[:, :width], load(f, 2)[:, :width]
        span = x.shape[1]
        right1 = pltpu.roll(x, span - 1, 1)[:, :width]
        left1 = pltpu.roll(x, 1, 1)[:, :width]
        right2 = pltpu.roll(x, span - 2, 1)[:, :width]
        left2 = pltpu.roll(x, 2, 1)[:, :width]
        x = x[:, :width]
        grad_q.append((up1 - down1) - 0.125 * (up2 - down2))
        grad_t.append((right1 - left1) - 0.125 * (right2 - left2))
        lap.append((up1 + down1) + (right1 + left1))
        centre.append(x)
    decay = STEP * damping + 4.0 * STEP * VISCOSITY
    results = []
    for i in range(FIELDS):
        flux = axial[i][0] * grad_q[0] + angular[i][0] * grad_t[0]
        for j in range(1, FIELDS):
            flux = flux + (axial[i][j] * grad_q[j] + angular[i][j] * grad_t[j])
        results.append((STEP * VISCOSITY) * lap[i] - flux - decay * centre[i])
    return centre, results


def ghost_layers(layers, coeff_ref):
    total = coeff_ref[0:1, :] * layers
    for distance in range(1, 2 * DONORS - 1):
        moved = pltpu.roll(layers, 256 - distance, 1)
        total = total + coeff_ref[distance : distance + 1, :] * moved
    return total


def pack_kernel(state_ref, damping_ref, first_ref, second_ref):
    even = lax.axis_index("sec") % 2 == 0
    group = lanes((PACK, 128)) // EDGE
    for a in range(FIELDS + 1):
        low = high = jnp.zeros((PACK, 128), jnp.float32)
        for j in range(128 // EDGE):
            rows = pl.ds(j * PACK, PACK)
            x = state_ref[0, a, rows, :] if a < FIELDS else damping_ref[0, rows, :]
            low = jnp.where(group == j, pltpu.roll(x, EDGE * j, 1) if j else x, low)
            shift = (EDGE * j + EDGE) % 128
            high = jnp.where(group == j, pltpu.roll(x, shift, 1) if shift else x, high)
        top = state_ref[0, a, 248:256, :] if a < FIELDS else damping_ref[0, 248:256, :]
        first_ref[a, 0:PACK, :] = jnp.where(even, high, low)
        second_ref[a, 0:PACK, :] = jnp.where(even, low, high)
        first_ref[a, PACK : PACK + 8, :] = top
        second_ref[a, PACK : PACK + 8, :] = top


def neighbours(even, first_ref, second_ref, a, rows):
    one = first_ref[jnp.where(even, 1, 0), a, rows, :]
    two = second_ref[jnp.where(even, 0, 1), a, rows, :]
    return jnp.where(even, one, two), jnp.where(even, two, one)


def edge_kernel(
    first_ref, second_ref, state_ref, damping_ref, weight_ref, offset_ref,
    rows_b_ref, rows_c_ref, send_ref, strip_ref, coeff_ref,
):
    sec = lax.axis_index("sec")
    grp = lax.axis_index("grp")
    even = sec % 2 == 0
    lane = lanes((8, 128))
    for a in range(FIELDS + 1):
        here = (lambda r: state_ref[0, a, r, :]) if a < FIELDS else (lambda r: damping_ref[0, r, :])
        right, left = neighbours(even, first_ref, second_ref, a, slice(PACK, PACK + 8))
        side = jnp.where(lane < WIDE, right, jnp.where(lane >= 128 - EDGE, left, 0.0))
        high = jnp.concatenate([here(slice(248, 256)), side], axis=1)
        right, left = neighbours(even, first_ref, second_ref, a, slice(0, 8))
        left = pltpu.roll(left, 128 - EDGE, 1)
        side = jnp.where(lane < EDGE, right, jnp.where(lane >= 128 - EDGE, left, 0.0))
        low = jnp.concatenate([here(slice(0, 8)), side], axis=1)
        rows_b_ref[a] = jnp.where(grp % 2 == 0, high, low)
        rows_c_ref[a] = jnp.where(grp == 2, low, high)
        strip_ref[a] = high
        if a < FIELDS:
            send_ref[2 * a : 2 * a + 1, :] = high[7:8, :]
            send_ref[2 * a + 1 : 2 * a + 2, :] = high[6:7, :]
    send_ref[10:16, :] = jnp.zeros((6, 256), jnp.float32)

    sectors = weight_ref.shape[1] // 128

    def window(ref, which):
        start = pl.multiple_of(((sec + which + sectors) % sectors) * 128, 128)
        return ref[:, pl.ds(start, 128)]

    def extended(ref):
        near, right, left = (window(ref, k) for k in (0, 1, -1))
        side = jnp.where(lanes(right.shape) < 64, right, left)
        return jnp.concatenate([near, side], axis=1)

    weight = extended(weight_ref)
    total = weight[0:1] + weight[1:2] + weight[2:3] + weight[3:4]
    weight = weight / total
    offset = extended(offset_ref)
    for distance in range(2 * DONORS - 1):
        coeff = jnp.zeros((1, 256), jnp.float32)
        for k in range(DONORS):
            coeff = coeff + jnp.where(offset == distance - k, weight[k : k + 1], 0.0)
        coeff_ref[distance : distance + 1, :] = coeff
    coeff_ref[7:8, :] = jnp.zeros((1, 256), jnp.float32)


def strip_kernel(
    stage, axial_ref, angular_ref, coeff_ref, got_ref, strip_ref, *refs,
):
    if stage == 0:
        now_ref = strip_ref
        out_ref, ghost_ref, send_ref, rows_ref = refs
    else:
        now_ref, out_ref, ghost_ref, send_ref, rows_ref = refs
    matrices = scaled_matrices(axial_ref, angular_ref)
    ghost = ghost_layers(got_ref[1 - lax.axis_index("row")], coeff_ref)
    ghost_ref[...] = ghost
    for f in range(FIELDS):
        rows_ref[f, 0:8, :] = jnp.zeros((8, 256), jnp.float32)
        rows_ref[f, 8:16, :] = now_ref[f]
        rows_ref[f, 16:18, :] = ghost[2 * f : 2 * f + 2, :]
        rows_ref[f, 18:24, :] = jnp.zeros((6, 256), jnp.float32)
    centre, more = increments(
        lambda f, k: rows_ref[f, 8 + k : 16 + k, :], strip_ref[FIELDS], matrices, 256
    )
    for f in range(FIELDS):
        new = centre[f] + more[f]
        if stage == 1:
            new = 0.75 * strip_ref[f] + 0.25 * new
        out_ref[f] = new
        send_ref[2 * f : 2 * f + 1, :] = new[7:8, :]
        send_ref[2 * f + 1 : 2 * f + 2, :] = new[6:7, :]
    send_ref[10:16, :] = jnp.zeros((6, 256), jnp.float32)


def step_kernel(
    axial_ref, angular_ref, coeff_ref, got_ref, ghost0_ref, ghost1_ref,
    first_ref, second_ref, rows_b_ref, rows_c_ref, state_ref, damping_ref,
    out_ref, whole_ref, x_ref, y_ref, z_ref, d_ref,
):
    sec = lax.axis_index("sec")
    grp = lax.axis_index("grp")
    even = sec % 2 == 0
    lane = lanes((PACK, 128))
    matrices = scaled_matrices(axial_ref, angular_ref)
    ghost2 = ghost_layers(got_ref[1 - lax.axis_index("row")], coeff_ref)

    for a in range(FIELDS + 1):
        source = state_ref.at[0, a] if a < FIELDS else damping_ref.at[0]
        right, left = neighbours(even, first_ref, second_ref, a, slice(0, PACK))
        for j in range(128 // EDGE):
            r = pltpu.roll(right, 128 - EDGE * j, 1) if j else right
            l = pltpu.roll(left, (128 - EDGE - EDGE * j) % 128, 1) if j < 15 else left
            side = jnp.where(lane < EDGE, r, jnp.where(lane >= 128 - EDGE, l, 0.0))
            whole_ref[a, 0, 8 + PACK * j : 8 + PACK * (j + 1), :] = source[pl.ds(PACK * j, PACK), :]
            whole_ref[a, 1, 8 + PACK * j : 8 + PACK * (j + 1), :] = side
        rows_b, rows_c = rows_b_ref[a], rows_c_ref[a]
        low = jnp.where(grp % 2 == 1, rows_b, rows_c)
        low = jnp.where(grp == 0, 0.0, low)
        high = jnp.where(grp % 2 == 0, rows_b, rows_c)
        high = jnp.where(grp == 3, 0.0, high)
        for h in range(2):
            whole_ref[a, h, 0:8, :] = low[:, 128 * h : 128 * (h + 1)]
            whole_ref[a, h, 264:272, :] = high[:, 128 * h : 128 * (h + 1)]
        for i in range(-REACH, 32 + REACH):
            for h in range(2):
                rows = whole_ref[a, h, pl.ds(8 + i, 8, stride=32), :]
                if a < FIELDS:
                    x_ref[a, i + REACH, :, 128 * h : 128 * (h + 1)] = rows
                else:
                    d_ref[i + REACH, :, 128 * h : 128 * (h + 1)] = rows

    def outer(ref, ghost, reach):
        @pl.when(grp == 3)
        def _():
            for f in range(FIELDS):
                for m in range(2):
                    ref[f, REACH + 32 + m, 7:8, :] = ghost[2 * f + m : 2 * f + m + 1, :]

        @pl.when(grp == 0)
        def _():
            for f in range(FIELDS):
                for i in range(-reach, 0):
                    ref[f, REACH + i, 0:1, :] = jnp.zeros((1, 256), jnp.float32)

    def block(ref, i, width):
        return increments(lambda f, k: ref[f, i + k], d_ref[i][:, :width], matrices, width)

    outer(x_ref, ghost0_ref[...], 0)

    @pl.loop(REACH - 4, REACH + 36)
    def _(i):
        centre, more = block(x_ref, i, 256)
        for f in range(FIELDS):
            y_ref[f, i] = centre[f] + more[f]

    outer(y_ref, ghost1_ref[...], 4)

    @pl.loop(REACH - 2, REACH + 34)
    def _(i):
        centre, more = block(y_ref, i, 256)
        for f in range(FIELDS):
            z_ref[f, i] = 0.75 * x_ref[f, i] + 0.25 * (centre[f] + more[f])

    outer(z_ref, ghost2, 2)

    @pl.loop(REACH, REACH + 32)
    def _(i):
        centre, more = block(z_ref, i, 128)
        for f in range(FIELDS):
            new = x_ref[f, i][:, :128] / 3.0 + (2.0 / 3.0) * (centre[f] + more[f])
            out_ref[0, f, pl.ds(i - REACH, 8, stride=32), :] = new


def call(kernel, in_specs, out_shapes, scratch=()):
    return pl.pallas_call(
        kernel,
        in_specs=in_specs,
        out_specs=[VMEM] * len(out_shapes),
        out_shape=[jax.ShapeDtypeStruct(s, jnp.float32) for s in out_shapes],
        scratch_shapes=list(scratch),
        compiler_params=pltpu.CompilerParams(vmem_limit_bytes=48 * 1024 * 1024),
    )


def solution(mesh):
    groups, sectors = mesh.shape["grp"], mesh.shape["sec"]

    def device(row, grp, sec):
        return (row * groups + grp) * sectors + sec % sectors

    everywhere = [(r, g) for r in range(2) for g in range(groups)]
    cores = [
        [device(r, g, c), device(r, g, c + 1)] for r, g in everywhere for c in range(0, sectors, 2)
    ]
    chips = [
        [device(r, g, c), device(r, g, c + 1)] for r, g in everywhere for c in range(1, sectors, 2)
    ]

    def swap(lows):
        pairs = []
        for r in range(2):
            for g in lows:
                for c in range(sectors):
                    one, two = device(r, g, c), device(r, g + 1, c)
                    pairs += [(one, two), (two, one)]
        return pairs

    def across(shift):
        pairs = [[device(0, groups - 1, c), device(1, groups - 1, c + shift)] for c in range(sectors)]
        return pairs + [
            [device(r, g, c), device(r, g, c + 1)]
            for r, g in everywhere
            if g < groups - 1
            for c in range(0, sectors, 2)
        ]

    def gather(x, members):
        return lax.all_gather(x, AXES, axis_index_groups=members)

    def moved(got, direction):
        row, even = lax.axis_index("row"), lax.axis_index("sec") % 2 == 0
        mine = jnp.where(row == 0, got[1], got[0])
        one, two = gather(mine, cores), gather(mine, chips)
        ahead = jnp.where(even, one[1], two[1])
        behind = jnp.where(even, two[0], one[0])
        result = jnp.where((row == 0) == (direction > 0), ahead, behind)
        return jnp.stack([result, result])

    def branch(shift):
        if shift == sectors - 2:
            return lambda x: moved(gather(x, across(sectors - 1)), -1)
        if shift % 2 == 1 and shift != sectors - 1:
            return lambda x: moved(gather(x, across(shift - 1)), 1)
        return lambda x: gather(x, across(shift))

    branches = [branch(s) for s in range(sectors)]

    def exchange(x, shift):
        return lax.switch(shift, branches, x)

    def shards(state, damping, jac_axial, jac_angular, section_shift, donor_offset, match_weight):
        arrays = FIELDS + 1
        first, second = call(pack_kernel, [VMEM] * 2, [(arrays, PACK + 8, 128)] * 2)(state, damping)
        first = gather(first, cores)
        second = gather(second, chips)
        rows_b, rows_c, send, strip, coeff = call(
            edge_kernel, [VMEM] * 6, [(arrays, 8, 256)] * 2 + [(16, 256), (arrays, 8, 256), (8, 256)]
        )(first, second, state, damping, match_weight, donor_offset[None, :])
        rows_b = lax.ppermute(rows_b, AXES, swap((0, 2)))
        rows_c = lax.ppermute(rows_c, AXES, swap((1,)))
        strip_out = [(FIELDS, 8, 256), (16, 256), (16, 256)]
        rows = [pltpu.VMEM((FIELDS, 24, 256), jnp.float32)]

        got = exchange(send, section_shift[0])
        strip1, ghost0, send = call(
            functools.partial(strip_kernel, 0), [SMEM] * 2 + [VMEM] * 3, strip_out, rows
        )(jac_axial, jac_angular, coeff, got, strip)
        got = exchange(send, section_shift[1])
        _, ghost1, send = call(
            functools.partial(strip_kernel, 1), [SMEM] * 2 + [VMEM] * 4, strip_out, rows
        )(jac_axial, jac_angular, coeff, got, strip, strip1)
        got = exchange(send, section_shift[2])
        depth = 32 + 2 * REACH
        fields = pltpu.VMEM((FIELDS, depth, 8, 256), jnp.float32)
        (out,) = call(
            step_kernel,
            [SMEM] * 2 + [VMEM] * 10,
            [(1, FIELDS, 256, 128)],
            [pltpu.VMEM((arrays, 2, 272, 128), jnp.float32)]
            + [fields] * 3
            + [pltpu.VMEM((depth, 8, 256), jnp.float32)],
        )(jac_axial, jac_angular, coeff, got, ghost0, ghost1, first, second, rows_b, rows_c, state, damping)
        return out

    return jax.shard_map(
        shards,
        mesh=mesh,
        in_specs=(
            P("row", None, "grp", "sec"),
            P("row", "grp", "sec"),
            P("row", None, None),
            P("row", None, None),
            P(),
            P(),
            P(),
        ),
        out_specs=P("row", None, "grp", "sec"),
        check_vma=False,
    )
```

time: 372 us -> 82.2 us (0.22); the launches traced: 367 us -> 81.8 us
  blocking collectives: 183 us -> 52.7 us
  other arithmetic: 103 us -> 0.02 us
  starting transfers between devices: 55.8 us -> 3.53 us
  Pallas kernels: 0 us -> 20 us
  local copies, waits for them, and re-layouts: 21.2 us -> 3.35 us
    all_gather x3 -> x7, blocking collectives: 183 us -> 52.7 us  [gather(): return lax.all_gather(x, AXES, axis_index_groups=members)]
    unnamed x24 -> x0, other arithmetic: 76.2 us -> none
    ppermute x15 -> x2, starting transfers between devices: 55.8 us -> 3.53 us  [the longest x1 2.86 us: shards(): rows_b = lax.ppermute(rows_b, AXES, swap((0, 2)))]
    pallas_call x0 -> x5, Pallas kernels: none -> 20 us  [the longest x1 17.1 us: shards(): call(step_kernel, [SMEM] * 2 + [VMEM] * 10, [(1, FIELDS, 256, 128)], [plt...]
    another operation x9 -> x1, other arithmetic: 18.3 us -> 0.01 us  [moved(): return jnp.stack([result, result])]
    gather x24 -> x0, local copies, waits for them, and re-layouts: 10 us -> none  [interface(): total = total + local_weights[donor] * jnp.take(window, index, axis=2)]
    slice x23 -> x1, local copies, waits for them, and re-layouts: 8.38 us -> 0.66 us  [shards(): got = exchange(send, section_shift[0])]
    div x4 -> x0, other arithmetic: 4.42 us -> none  [the longest x3 4.41 us: stencil(): first = (8.0 * (window(1) - window(-1)) - (window(2) - window(-2))) / 12.0]
  transfers between devices with their start and end apart: 15 -> 2, of which waited for: 0 -> 0; matrix products, arithmetic and copies ran while one was open for 6% -> 1% of each run, Pallas kernels for 0% -> 3%
where the time goes in v1:
time: 82.2 us; the launch traced here: 81.8 us
  blocking collectives  52.7 us (64%)
  Pallas kernels  20 us (24%)
  starting transfers between devices  3.53 us (4%)
  local copies, waits for them, and re-layouts  3.35 us (4%)
  between operations  2.03 us (2%)
    all_gather x7, blocking collectives, gather(): return lax.all_gather(x, AXES, axis_index_groups=members)  52.7 us
    pallas_call x1, Pallas kernels, shards(): call(step_kernel, [SMEM] * 2 + [VMEM] * 10, [(1, FIELDS, 256, 128)], [plt...  17.1 us
    ppermute x1, starting transfers between devices, shards(): rows_b = lax.ppermute(rows_b, AXES, swap((0, 2)))  2.86 us
    unnamed x20, local copies, waits for them, and re-layouts  2.69 us
  transfers between devices with their start and end apart: 2, of which 0 were waited for; matrix products, arithmetic and copies ran while one was open for 1% of the time, Pallas kernels for 3%

profile of v1, /device:TPU:6, one launch (start us, length us, event | category | flops | bytes accessed | tf_op | source)
XLA Modules:
  0.0 81.8 jit_solution(9085865057731871917)
XLA Ops:
  0.0 1.1 %copy-done = f32[1,5,256,128]{3,2,1,0:T(8,128)S(1)} copy-done((f32[1,5,256,128]{3,2,1,0:T(8,128)S(1)}, f32[1,5,256,128]{3,2,1,0:T(8,128)}, u32[]{:S(2)}) %copy-start) | copy-done | bytes 655384
  1.1 0.9 %copy-done.2 = f32[1,256,128]{2,1,0:T(8,128)S(1)} copy-done((f32[1,256,128]{2,1,0:T(8,128)S(1)}, f32[1,256,128]{2,1,0:T(8,128)}, u32[]{:S(2)}) %copy-start.2) | copy-done | bytes 131096
  2.0 0.4 shard_map.73
  2.4 1.9 %all-gather.192 = f32[12,24,128]{2,1,0:T(8,128)S(1)} all-gather(f32[6,24,128]{2,1,0:T(8,128)S(1)} %get-tuple-element.404), channel_id=194, replica_groups={{0,1},{2,3},{4,5},{6,7},{8,9},{10,11},{12,13},{14,15},{16,17},{18,19},{..., dimensions={0}, use_global_device_ids=true | all-gather | bytes 221184 | tf_op jit(solution)/shard_map/all_gather | solution.py:301
  4.4 13.1 %all-gather.193 = f32[12,24,128]{2,1,0:T(8,128)S(1)} all-gather(f32[6,24,128]{2,1,0:T(8,128)S(1)} %get-tuple-element.405), channel_id=195, replica_groups={{1,2},{3,4},{5,6},{7,8},{9,10},{11,12},{13,14},{15,16},{17,18},{19,20},..., dimensions={0}, use_global_device_ids=true | all-gather | bytes 221184 | tf_op jit(solution)/shard_map/all_gather | solution.py:301
  17.4 0.1 shard_map.74
  17.5 2.9 %collective-permute-start = (f32[6,8,256]{2,1,0:T(8,128)S(1)}, f32[6,8,256]{2,1,0:T(8,128)S(1)}, u32[]{:S(2)}, u32[]{:S(2)}) collective-permute-start(f32[6,8,256]{2,1,0:T(8,128)S(1)} %get-tuple-element.414), channel_id=1, source_target_pairs={{0,64},{64,0},{1,65},{65,1},{2,66},{66,2},{3,67},{67,3},{4,68},{68... | collective-permute-start | bytes 147464 | tf_op jit(solution)/shard_map/ppermute | solution.py:332
  20.4 0.7 collective-permute-start.1
  21.1 0.7 fusion.192
  22.3 0.0 copy-start.7
  23.7 0.0 copy-start.8
  23.7 0.7 copy-done.8
  24.4 7.1 %conditional.3 = (f32[2,16,256]{2,1,0:T(8,128)S(1)}) conditional(s32[]{:T(128)} %bitcast.197, f32[16,256]{1,0:T(8,128)S(1)} %get-tuple-element.407, f32[16,256]{1,0:T(8,128)S(1)} %get-tuple-element.407, f32[16,256]{1,0:T(8,128)S(1)} %get-tuple-element.407, f32[16,256]{1,0:T(8,128)S(1)} %get-tuple-element.407, ...), branch_computations={%region_0.0_spmd, %region_1.2_spmd, %region_2.3_spmd, %region_3.4_... | conditional | flops 24595 | bytes 327873 | solution.py:322
  24.4 7.1 %all-gather.63 = f32[32,256]{1,0:T(8,128)S(1)} all-gather(f32[16,256]{1,0:T(8,128)S(1)} %param.63), channel_id=65, replica_groups={{192,511},{193,448},{194,449},{195,450},{196,451},{197,452},{198,453},{..., dimensions={0}, use_global_device_ids=true | all-gather | bytes 49152 | tf_op jit(solution)/shard_map/cond/branch_63_fun/all_gather | solution.py:301
  31.5 0.9 %shard_map.75 = (f32[5,8,256]{2,1,0:T(8,128)S(1)}, f32[16,256]{1,0:T(8,128)S(1)}, f32[16,256]{1,0:T(8,128)S(1)}) custom-call(f32[1,5,5]{2,1,0:T(8,128)S(1)} %copy.18.axial_ref, f32[1,5,5]{2,1,0:T(8,128)S(1)} %copy.19.angular_ref, f32[8,256]{1,0:T(8,128)S(1)} %get-tuple-element.406.coeff_ref, f32[2,16,256]{2,1,0:T(8,128)S(1)} %get-tuple-element.419.got_ref, ...), custom_call_target="tpu_custom_call" | custom-call | tf_op jit(solution)/shard_map/pallas_call | solution.py:338
  32.4 15.8 %conditional.4 = (f32[2,16,256]{2,1,0:T(8,128)S(1)}) conditional(s32[]{:T(128)} %bitcast.196, f32[16,256]{1,0:T(8,128)S(1)} %get-tuple-element.409, f32[16,256]{1,0:T(8,128)S(1)} %get-tuple-element.409, f32[16,256]{1,0:T(8,128)S(1)} %get-tuple-element.409, f32[16,256]{1,0:T(8,128)S(1)} %get-tuple-element.409, ...), branch_computations={%region_64.65_spmd, %region_65.66_spmd, %region_66.67_spmd, %regio... | conditional | flops 24595 | bytes 327873 | solution.py:322
  32.6 15.5 %all-gather.96 = f32[32,256]{1,0:T(8,128)S(1)} all-gather(f32[16,256]{1,0:T(8,128)S(1)} %param.96), channel_id=98, replica_groups={{192,480},{193,481},{194,482},{195,483},{196,484},{197,485},{198,486},{..., dimensions={0}, use_global_device_ids=true | all-gather | bytes 49152 | tf_op jit(solution)/shard_map/cond/branch_32_fun/all_gather | solution.py:301
  48.2 1.5 %shard_map.76 = (f32[5,8,256]{2,1,0:T(8,128)}, f32[16,256]{1,0:T(8,128)S(1)}, f32[16,256]{1,0:T(8,128)S(1)}) custom-call(f32[1,5,5]{2,1,0:T(8,128)S(1)} %copy.18.axial_ref, f32[1,5,5]{2,1,0:T(8,128)S(1)} %copy.19.angular_ref, f32[8,256]{1,0:T(8,128)S(1)} %get-tuple-element.406.coeff_ref, f32[2,16,256]{2,1,0:T(8,128)S(1)} %get-tuple-element.420.got_ref, ...), custom_call_target="tpu_custom_call" | custom-call | tf_op jit(solution)/shard_map/pallas_call | solution.py:342
  49.7 15.1 %conditional.5 = (f32[2,16,256]{2,1,0:T(8,128)S(1)}) conditional(s32[]{:T(128)} %bitcast.195, f32[16,256]{1,0:T(8,128)S(1)} %get-tuple-element.411, f32[16,256]{1,0:T(8,128)S(1)} %get-tuple-element.411, f32[16,256]{1,0:T(8,128)S(1)} %get-tuple-element.411, f32[16,256]{1,0:T(8,128)S(1)} %get-tuple-element.411, ...), branch_computations={%region_128.129_spmd, %region_129.130_spmd, %region_130.131_spmd, ... | conditional | flops 24595 | bytes 327873 | solution.py:322
  49.7 7.3 %all-gather.190 = f32[32,256]{1,0:T(8,128)S(1)} all-gather(f32[16,256]{1,0:T(8,128)S(1)} %param.190), channel_id=192, replica_groups={{192,511},{193,448},{194,449},{195,450},{196,451},{197,452},{198,453},{..., dimensions={0}, use_global_device_ids=true | all-gather | bytes 49152 | tf_op jit(solution)/shard_map/cond/branch_62_fun/all_gather | solution.py:301
  56.9 1.8 %all-gather.384 = f32[32,256]{1,0:T(8,128)S(1)} all-gather(f32[16,256]{1,0:T(8,128)S(1)} %slice_select_fusion.287), channel_id=386, replica_groups={{0,1},{2,3},{4,5},{6,7},{8,9},{10,11},{12,13},{14,15},{16,17},{18,19},{..., dimensions={0}, use_global_device_ids=true | all-gather | bytes 49152 | tf_op jit(solution)/shard_map/cond/branch_62_fun/all_gather | solution.py:301
  58.8 5.9 %all-gather.385 = f32[32,256]{1,0:T(8,128)S(1)} all-gather(f32[16,256]{1,0:T(8,128)S(1)} %slice_select_fusion.287), channel_id=387, replica_groups={{1,2},{3,4},{5,6},{7,8},{9,10},{11,12},{13,14},{15,16},{17,18},{19,20},..., dimensions={0}, use_global_device_ids=true | all-gather | bytes 49152 | tf_op jit(solution)/shard_map/cond/branch_62_fun/all_gather | solution.py:301
  64.7 0.0 collective-permute-done.rows_b_ref
  64.8 17.1 %shard_map.77 = f32[1,5,256,128]{3,2,1,0:T(8,128)} custom-call(f32[1,5,5]{2,1,0:T(8,128)S(1)} %copy.18.axial_ref, f32[1,5,5]{2,1,0:T(8,128)S(1)} %copy.19.angular_ref, f32[8,256]{1,0:T(8,128)S(1)} %get-tuple-element.406.coeff_ref, f32[2,16,256]{2,1,0:T(8,128)S(1)} %get-tuple-element.421.got_ref, f32[16,256]{1,0:T(8,128)S(1)} %get-tuple-element.412.ghost0_ref, ...), custom_call_target="tpu_custom_call" | custom-call | tf_op jit(solution)/shard_map/pallas_call | solution.py:348
  (19 shorter events, 0.0 us)
Async XLA Ops:
  0.0 1.1 %copy-start = (f32[1,5,256,128]{3,2,1,0:T(8,128)S(1)}, f32[1,5,256,128]{3,2,1,0:T(8,128)}, u32[]{:S(2)}) copy-start(f32[1,5,256,128]{3,2,1,0:T(8,128)} %state_ref.5) | copy-start | bytes 1966084
  1.1 0.9 %copy-start.2 = (f32[1,256,128]{2,1,0:T(8,128)S(1)}, f32[1,256,128]{2,1,0:T(8,128)}, u32[]{:S(2)}) copy-start(f32[1,256,128]{2,1,0:T(8,128)} %damping_ref.5) | copy-start | bytes 393220
  4.3 13.1 %copy-start.4 = (f32[4,8192]{1,0:T(4,128)S(1)}, f32[4,8192]{1,0:T(4,128)}, u32[]{:S(2)}) copy-start(f32[4,8192]{1,0:T(4,128)} %weight_ref.1) | copy-start | bytes 393220
  4.4 13.1 %copy-start.5 = (s32[8192]{0:T(1024)S(1)}, s32[8192]{0:T(1024)}, u32[]{:S(2)}) copy-start(s32[8192]{0:T(1024)} %param.204) | copy-start | bytes 98308
  17.5 3.5 %copy-start.6 = (s32[3]{0:T(128)S(1)}, s32[3]{0:T(128)}, u32[]{:S(2)}) copy-start(s32[3]{0:T(128)} %param.203) | copy-start | bytes 40
  17.5 47.2 %collective-permute-start = (f32[6,8,256]{2,1,0:T(8,128)S(1)}, f32[6,8,256]{2,1,0:T(8,128)S(1)}, u32[]{:S(2)}, u32[]{:S(2)}) collective-permute-start(f32[6,8,256]{2,1,0:T(8,128)S(1)} %get-tuple-element.414), channel_id=1, source_target_pairs={{0,64},{64,0},{1,65},{65,1},{2,66},{66,2},{3,67},{67,3},{4,68},{68... | collective-permute-start | bytes 147464 | tf_op jit(solution)/shard_map/ppermute | solution.py:332
  20.4 44.3 %collective-permute-start.1 = (f32[6,8,256]{2,1,0:T(8,128)S(1)}, f32[6,8,256]{2,1,0:T(8,128)S(1)}, u32[]{:S(2)}, u32[]{:S(2)}) collective-permute-start(f32[6,8,256]{2,1,0:T(8,128)S(1)} %get-tuple-element.415), channel_id=1, source_target_pairs={{64,128},{128,64},{65,129},{129,65},{66,130},{130,66},{67,131},{13... | collective-permute-start | bytes 147464 | tf_op jit(solution)/shard_map/ppermute | solution.py:333
  22.3 1.4 %copy-start.7 = (f32[1,5,5]{2,0,1:T(1,128)S(1)}, f32[1,5,5]{2,0,1:T(1,128)}, u32[]{:S(2)}) copy-start(f32[1,5,5]{2,0,1:T(1,128)} %param.201) | copy-start | bytes 304
  23.7 0.7 copy-start.8
  49.6 15.1 %copy-start.1 = (f32[1,5,256,128]{3,2,1,0:T(8,128)S(1)}, f32[1,5,256,128]{3,2,1,0:T(8,128)}, u32[]{:S(2)}) copy-start(f32[1,5,256,128]{3,2,1,0:T(8,128)} %state_ref.5) | copy-start | bytes 1966084
  49.6 15.1 %copy-start.3 = (f32[1,256,128]{2,1,0:T(8,128)S(1)}, f32[1,256,128]{2,1,0:T(8,128)}, u32[]{:S(2)}) copy-start(f32[1,256,128]{2,1,0:T(8,128)} %damping_ref.5) | copy-start | bytes 393220

commit v2 on v0

v2 whole, which is shorter than its diff:
```python
import functools

import jax
import jax.numpy as jnp
from jax import lax
from jax.experimental import pallas as pl
from jax.experimental.pallas import tpu as pltpu
from jax.sharding import PartitionSpec as P

DONORS = 4
FIELDS = 5
STEP = 0.3
VISCOSITY = 0.05
AXES = ("row", "grp", "sec")

EDGE = 8
WIDE = 24
SECTORS = 64
ROUTE = (4,)
UNROLL = 4
REACH = 6

VMEM = pl.BlockSpec(memory_space=pltpu.VMEM)
ANY = pl.BlockSpec(memory_space=pl.ANY)
HBM = pl.BlockSpec(memory_space=pltpu.HBM)
SMEM = pl.BlockSpec(memory_space=pltpu.SMEM)


def lanes(shape):
    return lax.broadcasted_iota(jnp.int32, shape, len(shape) - 1)


def unique(i, j):
    i, j = min(i, j), max(i, j)
    return i * FIELDS - i * (i - 1) // 2 + j - i


ENTRIES = FIELDS * (FIELDS + 1) // 2


def advance(x, up1, down1, up2, down2, right1, left1, right2, left2, damping, matrices_ref):
    fields = range(FIELDS)
    grad_q = [(up1[f] - down1[f]) - 0.125 * (up2[f] - down2[f]) for f in fields]
    grad_t = [(right1[f] - left1[f]) - 0.125 * (right2[f] - left2[f]) for f in fields]
    keep = (1.0 - 4.0 * STEP * VISCOSITY) - STEP * damping
    results = []
    for i in fields:
        flux = None
        for j in fields:
            term = matrices_ref[unique(i, j)] * grad_q[j] + matrices_ref[ENTRIES + unique(i, j)] * grad_t[j]
            flux = term if flux is None else flux + term
        lap = (up1[i] + down1[i]) + (right1[i] + left1[i])
        results.append(keep * x[i] + ((STEP * VISCOSITY) * lap - flux))
    return results


def turned(near, side, lane):
    result = []
    for shift in (127, 1, 126, 2):
        one, two = pltpu.roll(near, shift, 1), pltpu.roll(side, shift, 1)
        inner = lane < shift if shift > 64 else lane >= shift
        result.append((jnp.where(inner, one, two), jnp.where(inner, two, one)))
    return result


def both(load, damping, matrices_ref, sides):
    fields = range(FIELDS)
    lane = lanes((8, 128))
    turns = [turned(load(f, 0, 0), load(f, 0, 1), lane) for f in fields]
    return [
        advance(
            [load(f, 0, h) for f in fields],
            *([load(f, k, h) for f in fields] for k in (1, -1, 2, -2)),
            *([turns[f][n][h] for f in fields] for n in range(4)),
            damping(h),
            matrices_ref,
        )
        for h in range(sides)
    ]


def ghost_layers(layers, coeff_ref):
    total = coeff_ref[0:1, :] * layers
    for distance in range(1, 2 * DONORS - 1):
        moved = pltpu.roll(layers, 256 - distance, 1)
        total = total + coeff_ref[distance : distance + 1, :] * moved
    return total


def spot(a):
    return 64 * (a // 4), EDGE * (a % 4)


def pack_kernel(
    state_ref, damping_ref, axial_ref, angular_ref, shift_ref,
    first_ref, second_ref, held_ref, own_ref, matrices_ref, route_ref, jac_ref, three_ref, sems,
):
    count = FIELDS + 1
    copies = []
    for a in range(count):
        source = state_ref.at[0, a] if a < FIELDS else damping_ref.at[0]
        copies.append(pltpu.make_async_copy(source, held_ref.at[a], sems.at[a]))
    for n, ref in enumerate((axial_ref, angular_ref)):
        copies.append(pltpu.make_async_copy(ref, jac_ref.at[n], sems.at[count + n]))
    copies.append(pltpu.make_async_copy(shift_ref, three_ref, sems.at[count + 2]))
    for copy in reversed(copies):
        copy.start()
    even = lax.axis_index("sec") % 2 == 0
    lane = lanes((8, 128))

    copies[count + 2].wait()
    half, last = SECTORS // 2, SECTORS - 1
    s0, s1, s2 = three_ref[0], three_ref[1], three_ref[2]
    at_half = jnp.where(s0 == half, 0, jnp.where(s1 == half, 1, 2))
    at_last = jnp.where(s0 == last, 0, jnp.where(s1 == last, 1, 2))
    free = 3 - at_half - at_last
    shift = jnp.where(free == 0, s0, jnp.where(free == 1, s1, s2))
    odd = shift & 1
    route_ref[0] = 2 * at_half + at_last - jnp.where(at_last > at_half, 1, 0)
    route_ref[1] = jnp.where(shift >= last - 1, half - 1, lax.shift_right_logical(shift, 1))
    route_ref[2] = jnp.where(odd == 0, jnp.where(shift == last - 1, 0, 1), jnp.where(shift == last, 1, 0))
    route_ref[3] = jnp.where(shift == last - 1, 1, 0)

    scale = STEP * 2.0 / 3.0 * 0.5
    for n in range(2):
        copies[count + n].wait()
        for i in range(FIELDS):
            for j in range(i, FIELDS):
                entry = scale * (jac_ref[n, i, :, j : j + 1] + jac_ref[n, j, :, i : i + 1])
                matrices_ref[ENTRIES * n + unique(i, j)] = jnp.broadcast_to(entry, (8, 128))

    for b in range(2):
        arrays = range(4 * b, min(4 * b + 4, count))
        for a in arrays:
            copies[a].wait()
        for i in range(8):
            low = high = jnp.zeros((8, 128), jnp.float32)
            for a in arrays:
                for k in range(4):
                    x = held_ref[a, pl.ds(8 * k + i, 8, stride=32), :]
                    place = 32 * k + spot(a)[1]
                    here = (lane >= place) & (lane < place + EDGE)
                    low = jnp.where(here, pltpu.roll(x, place, 1) if place else x, low)
                    shift = (place + EDGE) % 128
                    high = jnp.where(here, pltpu.roll(x, shift, 1) if shift else x, high)
            rows = slice(64 * b + 8 * i, 64 * b + 8 * i + 8)
            own_ref[0, rows, :] = low
            own_ref[1, rows, :] = high
            first_ref[rows, :] = jnp.where(even, high, low)
            second_ref[rows, :] = jnp.where(even, low, high)
        tops = jnp.zeros((8, 128), jnp.float32)
        for a in arrays:
            top, place = held_ref[a, 248:256, :], 32 * (a % 4)
            wide = (lane >= place) & (lane < place + WIDE)
            tops = jnp.where(wide, pltpu.roll(top, place, 1) if place else top, tops)
            narrow = (lane >= place + WIDE) & (lane < place + 32)
            shift = (place + 32) % 128
            tops = jnp.where(narrow, pltpu.roll(top, shift, 1) if shift else top, tops)
        first_ref[128 + 8 * b : 136 + 8 * b, :] = tops
        second_ref[128 + 8 * b : 136 + 8 * b, :] = tops


def neighbours(even, first_ref, second_ref, rows):
    one = first_ref[jnp.where(even, 1, 0), rows, :]
    two = second_ref[jnp.where(even, 0, 1), rows, :]
    return jnp.where(even, one, two), jnp.where(even, two, one)


def rotate(x, shift):
    shift %= 128
    return pltpu.roll(x, shift, 1) if shift else x


def edge_kernel(
    first_ref, second_ref, held_ref, weight_ref, offset_ref,
    rows_b_ref, rows_c_ref, send_ref, strip_ref, coeff_ref,
):
    sec = lax.axis_index("sec")
    grp = lax.axis_index("grp")
    even = sec % 2 == 0
    lane = lanes((8, 128))

    def side(right, left, count):
        return jnp.where(lane < count, right, jnp.where(lane >= 128 - EDGE, left, 0.0))

    for a in range(FIELDS + 1):
        start, place = spot(a)
        right, left = neighbours(even, first_ref, second_ref, slice(128 + 8 * (a // 4), 136 + 8 * (a // 4)))
        top = 32 * (a % 4)
        high = jnp.concatenate(
            [held_ref[a, 248:256, :], side(rotate(right, -top), rotate(left, 96 - top), WIDE)], axis=1
        )
        right, left = neighbours(even, first_ref, second_ref, pl.ds(start, 8, stride=8))
        low = jnp.concatenate(
            [held_ref[a, 0:8, :], side(rotate(right, -place), rotate(left, -EDGE - place), EDGE)], axis=1
        )
        right, left = neighbours(even, first_ref, second_ref, pl.ds(start + 7, 8, stride=8))
        place = place + 64
        strip_ref[a, 0:8, 0:128] = held_ref[a, 240:248, :]
        strip_ref[a, 0:8, 128:256] = side(rotate(right, -place), rotate(left, -EDGE - place), EDGE)
        strip_ref[a, 8:16, :] = high
        rows_b_ref[a] = jnp.where(grp % 2 == 0, high, low)
        rows_c_ref[a] = jnp.where(grp == 2, low, high)
        if a < FIELDS:
            send_ref[2 * a : 2 * a + 1, :] = high[7:8, :]
            send_ref[2 * a + 1 : 2 * a + 2, :] = high[6:7, :]
    send_ref[10:16, :] = jnp.zeros((6, 256), jnp.float32)

    sectors = weight_ref.shape[1] // 128

    def window(ref, which):
        start = pl.multiple_of(((sec + which + sectors) % sectors) * 128, 128)
        return ref[:, pl.ds(start, 128)]

    def extended(ref):
        near, right, left = (window(ref, k) for k in (0, 1, -1))
        return jnp.concatenate([near, jnp.where(lanes(right.shape) < 64, right, left)], axis=1)

    weight = extended(weight_ref)
    total = weight[0:1] + weight[1:2] + weight[2:3] + weight[3:4]
    weight = weight / total
    offset = extended(offset_ref)
    for distance in range(2 * DONORS - 1):
        coeff = jnp.zeros((1, 256), jnp.float32)
        for k in range(DONORS):
            coeff = coeff + jnp.where(offset == distance - k, weight[k : k + 1], 0.0)
        coeff_ref[distance : distance + 1, :] = coeff
    coeff_ref[7:8, :] = jnp.zeros((1, 256), jnp.float32)


def layers_of(got_ref):
    return got_ref[...] if len(got_ref.shape) == 2 else got_ref[1 - lax.axis_index("row")]


def strip_stage(now_ref, got_ref, strip_ref, coeff_ref, matrices_ref, rows_ref, blocks, sides):
    ghost = ghost_layers(layers_of(got_ref), coeff_ref)
    for f in range(FIELDS):
        rows_ref[f, 0:8, :] = jnp.zeros((8, 256), jnp.float32)
        rows_ref[f, 8:24, :] = now_ref[f]
        rows_ref[f, 24:26, :] = ghost[2 * f : 2 * f + 2, :]
        rows_ref[f, 26:32, :] = jnp.zeros((6, 256), jnp.float32)

    def halves(h):
        return slice(128 * h, 128 * (h + 1))

    return [
        both(
            lambda f, k, h: rows_ref[f, 8 + 8 * b + k : 16 + 8 * b + k, halves(h)],
            lambda h: strip_ref[FIELDS, 8 * b : 8 * b + 8, halves(h)],
            matrices_ref,
            sides,
        )
        for b in blocks
    ]


def strip_kernel(stage, matrices_ref, coeff_ref, got_ref, strip_ref, *refs):
    now_ref, out_ref, send_ref, rows_ref = refs if stage else (strip_ref, *refs)
    new = strip_stage(now_ref, got_ref, strip_ref, coeff_ref, matrices_ref, rows_ref, (0, 1), 2)
    for b in range(2):
        for h in range(2):
            for f in range(FIELDS):
                place = f, slice(8 * b, 8 * b + 8), slice(128 * h, 128 * h + 128)
                value = new[b][h][f]
                if stage:
                    value = 0.75 * strip_ref[place] + 0.25 * value
                out_ref[place] = value
                if b:
                    send_ref[2 * f : 2 * f + 1, place[2]] = value[7:8, :]
                    send_ref[2 * f + 1 : 2 * f + 2, place[2]] = value[6:7, :]
    send_ref[10:16, :] = jnp.zeros((6, 256), jnp.float32)


def last_kernel(matrices_ref, coeff_ref, got_ref, strip_ref, now_ref, _, out_ref, rows_ref, new_ref, sem):
    ((new,),) = strip_stage(now_ref, got_ref, strip_ref, coeff_ref, matrices_ref, rows_ref, (1,), 1)
    for f in range(FIELDS):
        new_ref[f] = strip_ref[f, 8:16, 0:128] / 3.0 + (2.0 / 3.0) * new[f]

    @pl.when(lax.axis_index("grp") == 3)
    def _():
        copy = pltpu.make_async_copy(new_ref, out_ref.at[0, :, 248:256, :], sem)
        copy.start()
        copy.wait()


def block_kernel(
    matrices_ref, first_ref, second_ref, own_ref, rows_b_ref, rows_c_ref, held_ref,
    out_ref, x_ref, y_ref, z_ref, d_ref, gx_ref, gy_ref, gz_ref, ge_ref, gd_ref,
):
    sec = lax.axis_index("sec")
    grp = lax.axis_index("grp")
    even = sec % 2 == 0
    lane = lanes((8, 128))
    part = lane % 32
    row = lax.broadcasted_iota(jnp.int32, (8, 128), 0)

    def choose(far_left, own_left, own_right, far_right):
        return jnp.where(
            part < 16, jnp.where(part < 8, far_left, own_left), jnp.where(part < 24, own_right, far_right)
        )

    for a in range(FIELDS + 1):
        near = x_ref.at[a] if a < FIELDS else d_ref
        side = gx_ref.at[a] if a < FIELDS else gd_ref
        rows_b, rows_c = rows_b_ref[a], rows_c_ref[a]
        low = jnp.where(grp == 0, 0.0, jnp.where(grp % 2 == 1, rows_b, rows_c))
        high = jnp.where(grp == 3, 0.0, jnp.where(grp % 2 == 0, rows_b, rows_c))
        for i in range(32):
            near[REACH + i] = held_ref[a, pl.ds(i, 8, stride=32), :]
        for i in range(REACH):
            below = pltpu.roll(near[REACH + 32 - REACH + i], 1, 0)
            near[i] = jnp.where(row == 0, low[8 - REACH + i : 9 - REACH + i, 0:128], below)
            above = pltpu.roll(near[REACH + i], 7, 0)
            near[REACH + 32 + i] = jnp.where(row == 7, high[i : i + 1, 0:128], above)
        start, place = spot(a)
        for i in range(8):
            rows = slice(start + 8 * i, start + 8 * i + 8)
            right, left = neighbours(even, first_ref, second_ref, rows)
            side[REACH + i] = choose(
                rotate(left, -place),
                rotate(own_ref[0, rows, :], 8 - place),
                rotate(own_ref[1, rows, :], 16 - place),
                rotate(right, 24 - place),
            )
        low, high = (
            choose(rotate(h[:, 128:], 8), rotate(h[:, :128], 8), rotate(h[:, :128], 24), rotate(h[:, 128:], 24))
            for h in (low, high)
        )
        high = pltpu.roll(high, 96, 1)
        for i in range(REACH):
            below = pltpu.roll(side[REACH + 8 - REACH + i], 32, 1)
            below = jnp.where(lane < 32, pltpu.roll(below, 1, 0), below)
            edge = (row == 0) & (lane < 32)
            side[i] = jnp.where(edge, low[8 - REACH + i : 9 - REACH + i, :], below)
            above = pltpu.roll(side[REACH + i], 96, 1)
            above = jnp.where(lane >= 96, pltpu.roll(above, 7, 0), above)
            edge = (row == 7) & (lane >= 96)
            side[REACH + 8 + i] = jnp.where(edge, high[i : i + 1, :], above)

    def nothing_before(near, side, reach):
        @pl.when(grp == 0)
        def _():
            for f in range(FIELDS):
                for i in range(REACH - reach, REACH):
                    near[f, i, 0:1, :] = jnp.zeros((1, 128), jnp.float32)
                    side[f, i, 0:1, 0:32] = jnp.zeros((1, 32), jnp.float32)

    fields = range(FIELDS)

    def axial(ref, i):
        return ([ref[f, i + k] for f in fields] for k in (0, 1, -1, 2, -2))

    def turns(x):
        return ([pltpu.roll(v, shift, 1) for v in x] for shift in (127, 1, 126, 2))

    def near_stage(near, side_new, first, last, store):
        @pl.loop(REACH + first, REACH + last, unroll=UNROLL)
        def _(i):
            k = jnp.clip(lax.shift_right_arithmetic(i - REACH, 3), 0, 3)
            x, *others = axial(near, i)
            new = advance(x, *others, *turns(x), d_ref[i], matrices_ref)
            for f in fields:
                beside = side_new[f, i - 8 * k]
                low = pltpu.roll(beside, (120 - 32 * k) & 127, 1)
                high = pltpu.roll(beside, (104 - 32 * k) & 127, 1)
                new[f] = jnp.where(lane < 2, low, jnp.where(lane >= 126, high, new[f]))
            store(i, new)

    def side_stage(side, first, last, store):
        @pl.loop(REACH + first, REACH + last, unroll=2)
        def _(i):
            x, *others = axial(side, i)
            store(i, advance(x, *others, *turns(x), gd_ref[i], matrices_ref))

    def plain(ref):
        def store(i, new):
            for f in fields:
                ref[f, i] = new[f]

        return store

    def blended(old, weights, put):
        def store(i, new):
            for f in fields:
                put(f, i, weights[0] * old[f, i] + weights[1] * new[f])

        return store

    def into(ref):
        def put(f, i, value):
            ref[f, i] = value

        return put

    def out(f, i, value):
        out_ref[0, f, pl.ds(i - REACH, 8, stride=32), :] = value

    side_stage(gx_ref, -4, 12, plain(gy_ref))
    near_stage(x_ref, gy_ref, -4, 36, plain(y_ref))
    nothing_before(y_ref, gy_ref, 4)
    side_stage(gy_ref, -2, 10, plain(ge_ref))
    near_stage(y_ref, ge_ref, -2, 34, blended(x_ref, (0.75, 0.25), into(z_ref)))
    for i in range(REACH - 2, REACH + 10):
        for f in fields:
            gz_ref[f, i] = 0.75 * gx_ref[f, i] + 0.25 * ge_ref[f, i]
    nothing_before(z_ref, gz_ref, 2)
    side_stage(gz_ref, 0, 8, plain(ge_ref))
    near_stage(z_ref, ge_ref, 0, 32, blended(x_ref, (1.0 / 3.0, 2.0 / 3.0), out))


def call(kernel, in_specs, out_shapes, scratch=(), out_specs=None, flops=0, vmem=40, **options):
    return pl.pallas_call(
        kernel,
        in_specs=in_specs,
        out_specs=out_specs or [SMEM if s == ROUTE else VMEM for s in out_shapes],
        out_shape=[jax.ShapeDtypeStruct(s, jnp.int32 if s == ROUTE else jnp.float32) for s in out_shapes],
        scratch_shapes=list(scratch),
        compiler_params=pltpu.CompilerParams(vmem_limit_bytes=vmem * 1024 * 1024),
        cost_estimate=pl.CostEstimate(flops=flops, bytes_accessed=flops // 10, transcendentals=0) if flops else None,
        **options,
    )


def solution(mesh):
    groups, sectors = mesh.shape["grp"], mesh.shape["sec"]

    def device(row, grp, sec):
        return (row * groups + grp) * sectors + sec % sectors

    everywhere = [(r, g) for r in range(2) for g in range(groups)]
    cores = [
        [device(r, g, c), device(r, g, c + 1)] for r, g in everywhere for c in range(0, sectors, 2)
    ]
    chips = [
        [device(r, g, c), device(r, g, c + 1)] for r, g in everywhere for c in range(1, sectors, 2)
    ]

    def swap(lows):
        pairs = []
        for r in range(2):
            for g in lows:
                for c in range(sectors):
                    one, two = device(r, g, c), device(r, g + 1, c)
                    pairs += [(one, two), (two, one)]
        return pairs

    def across(shift):
        pairs = [[device(0, groups - 1, c), device(1, groups - 1, c + shift)] for c in range(sectors)]
        return pairs + [
            [device(r, g, c), device(r, g, c + 1)]
            for r, g in everywhere
            if g < groups - 1
            for c in range(0, sectors, 2)
        ]

    def gather(x, members):
        return lax.all_gather(x, AXES, axis_index_groups=members)

    half = sectors // 2
    opposite = [pair for one, two in across(half)[:sectors] for pair in ((one, two), (two, one))]

    def branch(shift):
        if shift == half:
            return lambda x: jnp.stack([lax.ppermute(x, AXES, opposite)] * 2)
        return lambda x: gather(x, across(shift))

    branches = [branch(s) for s in range(0, sectors - 2, 2)] + [branch(sectors - 1)]

    def moved(got, back):
        row, even = lax.axis_index("row"), lax.axis_index("sec") % 2 == 0
        mine = jnp.where(row == 0, got[1], got[0])
        one, two = gather(mine, cores), gather(mine, chips)
        ahead = jnp.where(even, one[1], two[1])
        behind = jnp.where(even, two[0], one[0])
        result = jnp.where((row == 0) != (back == 1), ahead, behind)
        return jnp.stack([result, result])

    def any_shift(send, nearest, exact, back):
        got = lax.switch(nearest, branches, send)
        return lax.switch(exact, [lambda got: moved(got, back), lambda got: got], got)

    arrays = FIELDS + 1
    strip_shape = (FIELDS, 16, 256)
    rows = pltpu.VMEM((FIELDS, 32, 256), jnp.float32)

    def variant(at_half, at_last):
        def run(
            nearest, exact, back, send,
            strip, coeff, matrices, first, second, own, rows_b, rows_c, held,
        ):
            rows_b = lax.ppermute(rows_b, AXES, swap((0, 2)))
            rows_c = lax.ppermute(rows_c, AXES, swap((1,)))
            now = ()
            for stage in range(3):
                if stage == at_half:
                    got = lax.ppermute(send, AXES, opposite)
                    near = (32 + 2 * REACH, 8, 128)
                    side = (8 + 2 * REACH, 8, 128)
                    shapes = [(FIELDS, *near)] * 3 + [near] + [(FIELDS, *side)] * 4 + [side]
                    send, rows_b = lax.optimization_barrier((send, rows_b))
                    (block,) = call(
                        block_kernel,
                        [VMEM] * 7,
                        [(1, FIELDS, 256, 128)],
                        [pltpu.VMEM(shape, jnp.float32) for shape in shapes],
                        flops=40_000_000,
                    )(matrices, first, second, own, rows_b, rows_c, held)
                    got, block = lax.optimization_barrier((got, block))
                elif stage == at_last:
                    got = gather(send, across(sectors - 1))
                else:
                    got = any_shift(send, nearest, exact, back)
                if stage < 2:
                    strip_now, send = call(
                        functools.partial(strip_kernel, stage),
                        [VMEM] * (4 + len(now)),
                        [strip_shape, (16, 256)],
                        [rows],
                    )(matrices, coeff, got, strip, *now)
                    now = (strip_now,)
            (out,) = call(
                last_kernel,
                [VMEM] * 5 + [ANY],
                [(1, FIELDS, 256, 128)],
                [rows, pltpu.VMEM((FIELDS, 8, 128), jnp.float32), pltpu.SemaphoreType.DMA],
                [ANY],
                input_output_aliases={5: 0},
            )(matrices, coeff, got, strip, *now, block)
            return out

        return run

    variants = [variant(i, j) for i in range(3) for j in range(3) if i != j]

    def shards(state, damping, jac_axial, jac_angular, section_shift, donor_offset, match_weight):
        first, second, held, own, matrices, route = call(
            pack_kernel,
            [HBM] * 5,
            [(144, 128)] * 2 + [(arrays, 256, 128), (2, 128, 128), (2 * ENTRIES, 8, 128), ROUTE],
            [
                pltpu.VMEM((2, FIELDS, 1, FIELDS), jnp.float32),
                pltpu.SMEM((3,), jnp.int32),
                pltpu.SemaphoreType.DMA((arrays + 3,)),
            ],
            vmem=58,
        )(state, damping, jnp.swapaxes(jac_axial, 0, 1), jnp.swapaxes(jac_angular, 0, 1), section_shift)
        which, nearest, exact, back = route[0], route[1], route[2], route[3]
        first = gather(first, cores)
        second = gather(second, chips)
        rows_b, rows_c, send, strip, coeff = call(
            edge_kernel,
            [VMEM] * 5,
            [(arrays, 8, 256)] * 2 + [(16, 256), (arrays, 16, 256), (8, 256)],
        )(first, second, held, match_weight, donor_offset[None, :])
        return lax.switch(
            which, variants, nearest, exact, back, send,
            strip, coeff, matrices, first, second, own, rows_b, rows_c, held,
        )

    return jax.shard_map(
        shards,
        mesh=mesh,
        in_specs=(
            P("row", None, "grp", "sec"),
            P("row", "grp", "sec"),
            P("row", None, None),
            P("row", None, None),
            P(),
            P(),
            P(),
        ),
        out_specs=P("row", None, "grp", "sec"),
        check_vma=False,
    )
```

time: 372 us -> 77.6 us (0.21); the launches traced: 367 us -> 77 us
  blocking collectives: 183 us -> 43.2 us
  other arithmetic: 103 us -> 0.02 us
  starting transfers between devices: 55.8 us -> 15.4 us
  local copies, waits for them, and re-layouts: 21.2 us -> 1.23 us
  Pallas kernels: 0 us -> 13.7 us
    all_gather x3 -> x6, blocking collectives: 183 us -> 43.2 us  [gather(): return lax.all_gather(x, AXES, axis_index_groups=members)]
    unnamed x24 -> x0, other arithmetic: 76.2 us -> none
    ppermute x15 -> x3, starting transfers between devices: 55.8 us -> 15.4 us  [the longest x1 12 us: run(): got = lax.ppermute(send, AXES, opposite)]
    another operation x9 -> x1, other arithmetic: 18.3 us -> 0.01 us  [moved(): return jnp.stack([result, result])]
    pallas_call x0 -> x6, Pallas kernels: none -> 13.7 us  [the longest x1 9.72 us: run(): call(block_kernel, [VMEM] * 7, [(1, FIELDS, 256, 128)], [pltpu.VMEM(shape...]
    gather x24 -> x0, local copies, waits for them, and re-layouts: 10 us -> none  [interface(): total = total + local_weights[donor] * jnp.take(window, index, axis=2)]
    slice x23 -> x1, local copies, waits for them, and re-layouts: 8.38 us -> 0.61 us  [shards(): which, nearest, exact, back = (route[0], route[1], route[2], route[3])]
    div x4 -> x0, other arithmetic: 4.42 us -> none  [the longest x3 4.41 us: stencil(): first = (8.0 * (window(1) - window(-1)) - (window(2) - window(-2))) / 12.0]
  transfers between devices with their start and end apart: 15 -> 3, of which waited for: 0 -> 0; matrix products, arithmetic and copies ran while one was open for 6% -> 0% of each run, Pallas kernels for 0% -> 13%
where the time goes in v2:
time: 77.6 us; the launch traced here: 77 us
  blocking collectives  43.2 us (56%)
  starting transfers between devices  15.4 us (20%)
  Pallas kernels  13.7 us (18%)
  loops' own time  2.56 us (3%)
  local copies, waits for them, and re-layouts  1.23 us (2%)
  between operations  0.95 us (1%)
    all_gather x6, blocking collectives, gather(): return lax.all_gather(x, AXES, axis_index_groups=members)  43.2 us
    ppermute x1, starting transfers between devices, run(): got = lax.ppermute(send, AXES, opposite)  12 us
    pallas_call x1, Pallas kernels, run(): call(block_kernel, [VMEM] * 7, [(1, FIELDS, 256, 128)], [pltpu.VMEM(shape...  9.72 us
    ppermute x1, starting transfers between devices, run(): rows_b = lax.ppermute(rows_b, AXES, swap((0, 2)))  2.74 us
    pallas_call x1, Pallas kernels, shards(): call(pack_kernel, [HBM] * 5, [(144, 128)] * 2 + [(arrays, 256, 128), (2,...  2.55 us
    another operation x1, loops' own time, shards(): lax.switch(which, variants, nearest, exact, back, send, strip, coeff, mat...  1.86 us
  transfers between devices with their start and end apart: 3, of which 0 were waited for; matrix products, arithmetic and copies ran while one was open for 0% of the time, Pallas kernels for 13%

profile of v2, /device:TPU:6, one launch (start us, length us, event | category | flops | bytes accessed | tf_op | source)
XLA Modules:
  0.0 77.0 jit_solution(5968190361359591421)
XLA Ops:
  0.0 2.5 %shard_map.79 = (f32[144,128]{1,0:T(8,128)}, f32[144,128]{1,0:T(8,128)}, f32[6,256,128]{2,1,0:T(8,128)S(1)}, f32[2,128,128]{2,1,0:T(8,128)S(1)}, f32[30,8,128]{2,1,0:T(8,128)S(1)}, /*index=5*/s32[4]{0:T(128)}) custom-call(f32[1,5,256,128]{3,2,1,0:T(8,128)} %state_ref.1, f32[1,256,128]{2,1,0:T(8,128)} %damping_ref.1, f32[5,1,5]{2,1,0:T(1,128)} %bitcast.420, ...), custom_call_target="tpu_custom_call" | custom-call | tf_op jit(solution)/shard_map/pallas_call | solution.py:536
  2.6 0.6 copy-done.3
  3.2 0.6 fusion.6
  4.5 2.3 %all-gather.192 = f32[288,128]{1,0:T(8,128)S(1)} all-gather(f32[144,128]{1,0:T(8,128)} %get-tuple-element.750), channel_id=194, replica_groups={{0,1},{2,3},{4,5},{6,7},{8,9},{10,11},{12,13},{14,15},{16,17},{18,19},{..., dimensions={0}, use_global_device_ids=true | all-gather | bytes 221184 | tf_op jit(solution)/shard_map/all_gather | solution.py:457
  6.8 13.1 %all-gather.193 = f32[288,128]{1,0:T(8,128)S(1)} all-gather(f32[144,128]{1,0:T(8,128)S(1)} %copy-done.2), channel_id=195, replica_groups={{1,2},{3,4},{5,6},{7,8},{9,10},{11,12},{13,14},{15,16},{17,18},{19,20},..., dimensions={0}, use_global_device_ids=true | all-gather | bytes 221184 | tf_op jit(solution)/shard_map/all_gather | solution.py:457
  19.8 0.0 copy-done.1
  19.8 0.1 shard_map.80
  20.0 56.8 %conditional.13 = (f32[1,5,256,128]{3,2,1,0:T(8,128)}) conditional(s32[]{:T(128)} %bitcast.200, (s32[]{:T(128)}, s32[]{:T(128)}, f32[16,256]{1,0:T(8,128)S(1)}, f32[6,8,256]{2,1,0:T(8,128)S(1)}, f32[6,8,256]{2,1,0:T(8,128)S(1)}, /*index=5*/f32[30,8,128]{2,1,0:T(8,128)S(1)}, f32[2,144,128]{2,1,0:T(8,128)S(1)}, ...), branch_computations={%region_0.35_spmd, %region_35.70_spmd, %region_70.105_spmd, %regio... | conditional | flops 40032792 | bytes 4901546 | solution.py:555
  20.0 2.7 %collective-permute-start.2 = (f32[6,8,256]{2,1,0:T(8,128)S(1)}, f32[6,8,256]{2,1,0:T(8,128)S(1)}, u32[]{:S(2)}, u32[]{:S(2)}) collective-permute-start(f32[6,8,256]{2,1,0:T(8,128)S(1)} %get-tuple-element.617), channel_id=1, source_target_pairs={{0,64},{64,0},{1,65},{65,1},{2,66},{66,2},{3,67},{67,3},{4,68},{68... | collective-permute-start | bytes 147464 | tf_op jit(solution)/shard_map/cond/branch_0_fun/ppermute | solution.py:491
  22.7 0.7 collective-permute-start.3
  23.4 12.0 %collective-permute-start.1 = (f32[16,256]{1,0:T(8,128)S(1)}, f32[16,256]{1,0:T(8,128)S(1)}, u32[]{:S(2)}, u32[]{:S(2)}) collective-permute-start(f32[16,256]{1,0:T(8,128)S(1)} %get-tuple-element.613), channel_id=1, source_target_pairs={{192,480},{480,192},{193,481},{481,193},{194,482},{482,194},{195,4... | collective-permute-start | bytes 49160 | tf_op jit(solution)/shard_map/cond/branch_0_fun/ppermute | solution.py:496
  36.6 0.0 collective-permute-done.2.rows_b_ref
  36.6 0.0 collective-permute-done.3.rows_c_ref
  36.6 9.7 %branch_0_fun.4._ = f32[1,5,256,128]{3,2,1,0:T(8,128)} custom-call(f32[30,8,128]{2,1,0:T(8,128)S(1)} %get-tuple-element.608.matrices_ref, f32[2,144,128]{2,1,0:T(8,128)S(1)} %get-tuple-element.614.first_ref, f32[2,144,128]{2,1,0:T(8,128)S(1)} %get-tuple-element.615.second_ref, f32[2,128,128]{2,1,0:T(8,128)S(1)} %get-tuple-element.616.own_ref, ...), custom_call_target="tpu_custom_call" | custom-call | flops 40000000 | bytes 4000000 | tf_op jit(solution)/shard_map/cond/branch_0_fun/pallas_call | solution.py:501
  46.4 0.0 collective-permute-done.1.got_ref
  46.4 0.2 branch_0_fun.5
  46.6 7.2 %all-gather.31 = f32[32,256]{1,0:T(8,128)S(1)} all-gather(f32[16,256]{1,0:T(8,128)S(1)} %get-tuple-element.623), channel_id=33, replica_groups={{192,511},{193,448},{194,449},{195,450},{196,451},{197,452},{198,453},{..., dimensions={0}, use_global_device_ids=true | all-gather | bytes 49152 | tf_op jit(solution)/shard_map/cond/branch_0_fun/all_gather | solution.py:457
  53.8 0.3 branch_0_fun.6
  54.0 13.0 %conditional = (f32[2,16,256]{2,1,0:T(8,128)S(1)}) conditional(s32[]{:T(128)} %clamp.29, f32[16,256]{1,0:T(8,128)S(1)} %get-tuple-element.625, f32[16,256]{1,0:T(8,128)S(1)} %get-tuple-element.625, f32[16,256]{1,0:T(8,128)S(1)} %get-tuple-element.625, f32[16,256]{1,0:T(8,128)S(1)} %get-tuple-element.625, ...), branch_computations={%region_1.0_spmd, %region_2.0_spmd, %region_3.0_spmd, %region_4.0_... | conditional | flops 8192 | bytes 114736 | solution.py:479
  54.1 12.9 %all-gather.21 = f32[32,256]{1,0:T(8,128)S(1)} all-gather(f32[16,256]{1,0:T(8,128)S(1)} %param.22), channel_id=23, replica_groups={{192,492},{193,493},{194,494},{195,495},{196,496},{197,497},{198,498},{..., dimensions={0}, use_global_device_ids=true | all-gather | bytes 49152 | tf_op jit(solution)/shard_map/cond/branch_0_fun/cond/branch_22_fun/all_gather | solution.py:457
  67.0 8.4 %conditional.1 = (f32[2,16,256]{2,1,0:T(8,128)S(1)}) conditional(s32[]{:T(128)} %clamp.28, (s32[]{:T(128)}, f32[2,16,256]{2,1,0:T(8,128)S(1)}) %tuple.625, f32[2,16,256]{2,1,0:T(8,128)S(1)} %get-tuple-element.771), branch_computations={%region_33.33_spmd, %region_34.34_spmd} | conditional | flops 24596 | bytes 278730 | solution.py:480
  67.6 6.0 %all_gather.875 = f32[2,16,256]{2,1,0:T(8,128)S(1)} all-gather(f32[1,16,256]{2,1,0:T(8,128)S(1)} %slice_select_fusion.2), channel_id=1, replica_groups={{1,2},{3,4},{5,6},{7,8},{9,10},{11,12},{13,14},{15,16},{17,18},{19,20},..., dimensions={0}, use_global_device_ids=true | all-gather | bytes 49152 | tf_op jit(solution)/shard_map/cond/branch_0_fun/cond/branch_0_fun/all_gather | solution.py:457
  73.6 1.8 %all_gather.874 = f32[2,16,256]{2,1,0:T(8,128)S(1)} all-gather(f32[1,16,256]{2,1,0:T(8,128)S(1)} %slice_select_fusion.2), channel_id=1, replica_groups={{0,1},{2,3},{4,5},{6,7},{8,9},{10,11},{12,13},{14,15},{16,17},{18,19},{..., dimensions={0}, use_global_device_ids=true | all-gather | bytes 49152 | tf_op jit(solution)/shard_map/cond/branch_0_fun/cond/branch_0_fun/all_gather | solution.py:457
  75.4 0.8 %branch_0_fun.7 = f32[1,5,256,128]{3,2,1,0:T(8,128)} custom-call(f32[30,8,128]{2,1,0:T(8,128)S(1)} %get-tuple-element.608.matrices_ref, f32[8,256]{1,0:T(8,128)S(1)} %get-tuple-element.609.coeff_ref, f32[2,16,256]{2,1,0:T(8,128)S(1)} %get-tuple-element.772.got_ref, f32[6,16,256]{2,1,0:T(8,128)S(1)} %get-tuple-element.622.strip_ref, ...), custom_call_target="tpu_custom_call", output_to_operand_aliasing={{}: (5, {})} | custom-call | tf_op jit(solution)/shard_map/cond/branch_0_fun/pallas_call | solution.py:521
  (9 shorter events, 0.0 us)
Async XLA Ops:
  2.6 0.6 copy-start.3
  4.5 2.3 %copy-start.2 = (f32[144,128]{1,0:T(8,128)S(1)}, f32[144,128]{1,0:T(8,128)}, u32[]{:S(2)}) copy-start(f32[144,128]{1,0:T(8,128)} %get-tuple-element.751) | copy-start | bytes 221188
  6.7 13.1 %copy-start = (f32[4,8192]{1,0:T(4,128)S(1)}, f32[4,8192]{1,0:T(4,128)}, u32[]{:S(2)}) copy-start(f32[4,8192]{1,0:T(4,128)} %weight_ref.1) | copy-start | bytes 393220
  6.8 13.1 %copy-start.1 = (s32[8192]{0:T(1024)S(1)}, s32[8192]{0:T(1024)}, u32[]{:S(2)}) copy-start(s32[8192]{0:T(1024)} %param.222) | copy-start | bytes 98308
  20.0 16.6 %collective-permute-start.2 = (f32[6,8,256]{2,1,0:T(8,128)S(1)}, f32[6,8,256]{2,1,0:T(8,128)S(1)}, u32[]{:S(2)}, u32[]{:S(2)}) collective-permute-start(f32[6,8,256]{2,1,0:T(8,128)S(1)} %get-tuple-element.617), channel_id=1, source_target_pairs={{0,64},{64,0},{1,65},{65,1},{2,66},{66,2},{3,67},{67,3},{4,68},{68... | collective-permute-start | bytes 147464 | tf_op jit(solution)/shard_map/cond/branch_0_fun/ppermute | solution.py:491
  22.7 13.9 %collective-permute-start.3 = (f32[6,8,256]{2,1,0:T(8,128)S(1)}, f32[6,8,256]{2,1,0:T(8,128)S(1)}, u32[]{:S(2)}, u32[]{:S(2)}) collective-permute-start(f32[6,8,256]{2,1,0:T(8,128)S(1)} %get-tuple-element.619), channel_id=1, source_target_pairs={{64,128},{128,64},{65,129},{129,65},{66,130},{130,66},{67,131},{13... | collective-permute-start | bytes 147464 | tf_op jit(solution)/shard_map/cond/branch_0_fun/ppermute | solution.py:492
  23.4 23.0 %collective-permute-start.1 = (f32[16,256]{1,0:T(8,128)S(1)}, f32[16,256]{1,0:T(8,128)S(1)}, u32[]{:S(2)}, u32[]{:S(2)}) collective-permute-start(f32[16,256]{1,0:T(8,128)S(1)} %get-tuple-element.613), channel_id=1, source_target_pairs={{192,480},{480,192},{193,481},{481,193},{194,482},{482,194},{195,4... | collective-permute-start | bytes 49160 | tf_op jit(solution)/shard_map/cond/branch_0_fun/ppermute | solution.py:496

commit v3 on v2

--- a/solution.py
+++ b/solution.py
@@ -16,8 +16,8 @@
 EDGE = 8
 WIDE = 24
 SECTORS = 64
-ROUTE = (4,)
-UNROLL = 4
+ROUTE = (1,)
+UNROLL = 8
 REACH = 6
 
 VMEM = pl.BlockSpec(memory_space=pltpu.VMEM)
@@ -93,7 +93,8 @@
 
 def pack_kernel(
     state_ref, damping_ref, axial_ref, angular_ref, shift_ref,
-    first_ref, second_ref, held_ref, own_ref, matrices_ref, route_ref, jac_ref, three_ref, sems,
+    first_ref, second_ref, held_ref, own_ref, matrices_ref,
+    which_ref, nearest_ref, exact_ref, back_ref, jac_ref, three_ref, sems,
 ):
     count = FIELDS + 1
     copies = []
@@ -116,10 +117,10 @@
     free = 3 - at_half - at_last
     shift = jnp.where(free == 0, s0, jnp.where(free == 1, s1, s2))
     odd = shift & 1
-    route_ref[0] = 2 * at_half + at_last - jnp.where(at_last > at_half, 1, 0)
-    route_ref[1] = jnp.where(shift >= last - 1, half - 1, lax.shift_right_logical(shift, 1))
-    route_ref[2] = jnp.where(odd == 0, jnp.where(shift == last - 1, 0, 1), jnp.where(shift == last, 1, 0))
-    route_ref[3] = jnp.where(shift == last - 1, 1, 0)
+    which_ref[0] = 2 * at_half + at_last - jnp.where(at_last > at_half, 1, 0)
+    nearest_ref[0] = jnp.where(shift >= last - 1, half - 1, lax.shift_right_logical(shift, 1))
+    exact_ref[0] = jnp.where(odd == 0, jnp.where(shift == last - 1, 0, 1), jnp.where(shift == last, 1, 0))
+    back_ref[0] = jnp.where(shift == last - 1, 1, 0)
 
     scale = STEP * 2.0 / 3.0 * 0.5
     for n in range(2):
@@ -367,7 +368,7 @@
             store(i, new)
 
     def side_stage(side, first, last, store):
-        @pl.loop(REACH + first, REACH + last, unroll=2)
+        @pl.loop(REACH + first, REACH + last, unroll=4)
         def _(i):
             x, *others = axial(side, i)
             store(i, advance(x, *others, *turns(x), gd_ref[i], matrices_ref))
@@ -533,10 +534,10 @@
     variants = [variant(i, j) for i in range(3) for j in range(3) if i != j]
 
     def shards(state, damping, jac_axial, jac_angular, section_shift, donor_offset, match_weight):
-        first, second, held, own, matrices, route = call(
+        first, second, held, own, matrices, *route = call(
             pack_kernel,
             [HBM] * 5,
-            [(144, 128)] * 2 + [(arrays, 256, 128), (2, 128, 128), (2 * ENTRIES, 8, 128), ROUTE],
+            [(144, 128)] * 2 + [(arrays, 256, 128), (2, 128, 128), (2 * ENTRIES, 8, 128)] + [ROUTE] * 4,
             [
                 pltpu.VMEM((2, FIELDS, 1, FIELDS), jnp.float32),
                 pltpu.SMEM((3,), jnp.int32),
@@ -544,7 +545,7 @@
             ],
             vmem=58,
         )(state, damping, jnp.swapaxes(jac_axial, 0, 1), jnp.swapaxes(jac_angular, 0, 1), section_shift)
-        which, nearest, exact, back = route[0], route[1], route[2], route[3]
+        which, nearest, exact, back = (r.reshape(()) for r in route)
         first = gather(first, cores)
         second = gather(second, chips)
         rows_b, rows_c, send, strip, coeff = call(

time: 77.6 us -> 67.7 us (0.87)
  blocking collectives: 43.2 us -> 36.8 us
  Pallas kernels: 13.7 us -> 12.2 us
  local copies, waits for them, and re-layouts: 1.23 us -> 0.01 us
    all_gather x6 -> x4, blocking collectives: 43.2 us -> 36.8 us  [gather(): return lax.all_gather(x, AXES, axis_index_groups=members)]
    pallas_call x1, Pallas kernels: 9.72 us -> 8.3 us  [run(): call(block_kernel, [VMEM] * 7, [(1, FIELDS, 256, 128)], [pltpu.VMEM(shape...]
  transfers between devices with their start and end apart: 3 -> 3, of which waited for: 0 -> 0; matrix products, arithmetic and copies ran while one was open for 0% -> 0% of each run, Pallas kernels for 13% -> 12%
where the time goes in v3:
time: 67.7 us; the launch traced here: 67.5 us
  blocking collectives  36.8 us (54%)
  starting transfers between devices  15.4 us (23%)
  Pallas kernels  12.2 us (18%)
  loops' own time  2.12 us (3%)
  between operations  0.88 us (1%)
    all_gather x4, blocking collectives, gather(): return lax.all_gather(x, AXES, axis_index_groups=members)  36.8 us
    ppermute x1, starting transfers between devices, run(): got = lax.ppermute(send, AXES, opposite)  12 us
    pallas_call x1, Pallas kernels, run(): call(block_kernel, [VMEM] * 7, [(1, FIELDS, 256, 128)], [pltpu.VMEM(shape...  8.3 us
    ppermute x1, starting transfers between devices, run(): rows_b = lax.ppermute(rows_b, AXES, swap((0, 2)))  2.74 us
    pallas_call x1, Pallas kernels, shards(): call(pack_kernel, [HBM] * 5, [(144, 128)] * 2 + [(arrays, 256, 128), (2,...  2.56 us
    another operation x1, loops' own time, shards(): lax.switch(which, variants, nearest, exact, back, send, strip, coeff, mat...  2.06 us
  transfers between devices with their start and end apart: 3, of which 0 were waited for; matrix products, arithmetic and copies ran while one was open for 0% of the time, Pallas kernels for 12%

profile of v3, /device:TPU:6, one launch (start us, length us, event | category | flops | bytes accessed | tf_op | source)
XLA Modules:
  0.0 67.5 jit_solution(11749250648354463868)
XLA Ops:
  0.0 2.6 %shard_map.79 = (f32[144,128]{1,0:T(8,128)}, f32[144,128]{1,0:T(8,128)}, f32[6,256,128]{2,1,0:T(8,128)S(1)}, f32[2,128,128]{2,1,0:T(8,128)S(1)}, f32[30,8,128]{2...) custom-call(f32[1,5,256,128]{3,2,1,0:T(8,128)} %state_ref.1, f32[1,256,128]{2,1,0:T(8,128)} %damping_ref.1, ...), custom_call_target="tpu_custom_call" | custom-call | tf_op jit(solution)/shard_map/pallas_call | solution.py:537
  3.2 0.0 copy-start.2
  3.2 2.3 %all-gather.192 = f32[288,128]{1,0:T(8,128)S(1)} all-gather(f32[144,128]{1,0:T(8,128)} %get-tuple-element.755), channel_id=194, replica_groups={{0,1},{2,3},{4,5},{6,7},{8,9},{10,11},{12,13},{14,15},{16,17},{18,19},{..., dimensions={0}, use_global_device_ids=true | all-gather | bytes 221184 | tf_op jit(solution)/shard_map/all_gather | solution.py:458
  5.5 0.0 copy-start
  5.5 0.0 copy-done.2
  5.5 0.0 copy-start.1
  5.5 13.1 %all-gather.193 = f32[288,128]{1,0:T(8,128)S(1)} all-gather(f32[144,128]{1,0:T(8,128)S(1)} %copy-done.2), channel_id=195, replica_groups={{1,2},{3,4},{5,6},{7,8},{9,10},{11,12},{13,14},{15,16},{17,18},{19,20},..., dimensions={0}, use_global_device_ids=true | all-gather | bytes 221184 | tf_op jit(solution)/shard_map/all_gather | solution.py:458
  18.6 0.0 copy-done
  18.6 0.0 copy-done.1
  18.6 0.1 shard_map.80
  18.7 48.6 %conditional.13 = (f32[1,5,256,128]{3,2,1,0:T(8,128)}) conditional(s32[]{:T(128)} %bitcast.200, (s32[]{:T(128)}, s32[]{:T(128)}, f32[16,256]{1,0:T(8,128)S(1)}, f32[6,8,256]{2,1,0:T(8,128)S(1)}, f32[6,8,256]{2,1,0:T(8,128)S(1)}, /*index=5*/f32[30,8,128]{2,1,0:T(8,128)S(1)}, f32[2,144,128]{2,1,0:T(8,128)S(1)}, ...), branch_computations={%region_0.35_spmd, %region_35.70_spmd, %region_70.105_spmd, %regio... | conditional | flops 40032792 | bytes 4901546 | solution.py:556
  18.7 2.7 %collective-permute-start.6 = (f32[6,8,256]{2,1,0:T(8,128)S(1)}, f32[6,8,256]{2,1,0:T(8,128)S(1)}, u32[]{:S(2)}, u32[]{:S(2)}) collective-permute-start(f32[6,8,256]{2,1,0:T(8,128)S(1)} %get-tuple-element.639), channel_id=1, source_target_pairs={{0,64},{64,0},{1,65},{65,1},{2,66},{66,2},{3,67},{67,3},{4,68},{68... | collective-permute-start | bytes 147464 | tf_op jit(solution)/shard_map/cond/branch_1_fun/ppermute | solution.py:492
  21.4 0.7 collective-permute-start.7
  22.1 12.0 %collective-permute-start.5 = (f32[16,256]{1,0:T(8,128)S(1)}, f32[16,256]{1,0:T(8,128)S(1)}, u32[]{:S(2)}, u32[]{:S(2)}) collective-permute-start(f32[16,256]{1,0:T(8,128)S(1)} %get-tuple-element.635), channel_id=1, source_target_pairs={{192,480},{480,192},{193,481},{481,193},{194,482},{482,194},{195,4... | collective-permute-start | bytes 49160 | tf_op jit(solution)/shard_map/cond/branch_1_fun/ppermute | solution.py:497
  35.4 0.0 collective-permute-done.6.rows_b_ref
  35.4 0.0 collective-permute-done.7.rows_c_ref
  35.4 8.3 %branch_1_fun.4._ = f32[1,5,256,128]{3,2,1,0:T(8,128)} custom-call(f32[30,8,128]{2,1,0:T(8,128)S(1)} %get-tuple-element.630.matrices_ref, f32[2,144,128]{2,1,0:T(8,128)S(1)} %get-tuple-element.636.first_ref, f32[2,144,128]{2,1,0:T(8,128)S(1)} %get-tuple-element.637.second_ref, f32[2,128,128]{2,1,0:T(8,128)S(1)} %get-tuple-element.638.own_ref, ...), custom_call_target="tpu_custom_call" | custom-call | flops 40000000 | bytes 4000000 | tf_op jit(solution)/shard_map/cond/branch_1_fun/pallas_call | solution.py:502
  43.7 0.0 collective-permute-done.5.got_ref
  43.7 0.2 branch_1_fun.5
  43.9 14.4 %conditional.2 = (f32[2,16,256]{2,1,0:T(8,128)S(1)}) conditional(s32[]{:T(128)} %clamp.31, f32[16,256]{1,0:T(8,128)S(1)} %get-tuple-element.645, f32[16,256]{1,0:T(8,128)S(1)} %get-tuple-element.645, f32[16,256]{1,0:T(8,128)S(1)} %get-tuple-element.645, f32[16,256]{1,0:T(8,128)S(1)} %get-tuple-element.645, ...), branch_computations={%region_36.36_spmd, %region_37.37_spmd, %region_38.38_spmd, %regio... | conditional | flops 8192 | bytes 114736 | solution.py:480
  44.0 14.3 %all-gather.50 = f32[32,256]{1,0:T(8,128)S(1)} all-gather(f32[16,256]{1,0:T(8,128)S(1)} %param.54), channel_id=52, replica_groups={{192,486},{193,487},{194,488},{195,489},{196,490},{197,491},{198,492},{..., dimensions={0}, use_global_device_ids=true | all-gather | bytes 49152 | tf_op jit(solution)/shard_map/cond/branch_1_fun/cond/branch_19_fun/all_gather | solution.py:458
  58.3 0.3 branch_1_fun.6
  58.6 7.2 %all-gather.63 = f32[32,256]{1,0:T(8,128)S(1)} all-gather(f32[16,256]{1,0:T(8,128)S(1)} %get-tuple-element.647), channel_id=65, replica_groups={{192,511},{193,448},{194,449},{195,450},{196,451},{197,452},{198,453},{..., dimensions={0}, use_global_device_ids=true | all-gather | bytes 49152 | tf_op jit(solution)/shard_map/cond/branch_1_fun/all_gather | solution.py:458
  65.7 0.8 %branch_1_fun.7 = f32[1,5,256,128]{3,2,1,0:T(8,128)} custom-call(f32[30,8,128]{2,1,0:T(8,128)S(1)} %get-tuple-element.630.matrices_ref, f32[8,256]{1,0:T(8,128)S(1)} %get-tuple-element.631.coeff_ref, f32[2,16,256]{2,1,0:T(8,128)S(1)} %bitcast.207, f32[6,16,256]{2,1,0:T(8,128)S(1)} %get-tuple-element.644.strip_ref, ...), custom_call_target="tpu_custom_call", output_to_operand_aliasing={{}: (5, {})} | custom-call | tf_op jit(solution)/shard_map/cond/branch_1_fun/pallas_call | solution.py:522
  (1 shorter events, 0.0 us)
Async XLA Ops:
  3.2 2.3 %copy-start.2 = (f32[144,128]{1,0:T(8,128)S(1)}, f32[144,128]{1,0:T(8,128)}, u32[]{:S(2)}) copy-start(f32[144,128]{1,0:T(8,128)} %get-tuple-element.756) | copy-start | bytes 221188
  5.5 13.1 %copy-start = (f32[4,8192]{1,0:T(4,128)S(1)}, f32[4,8192]{1,0:T(4,128)}, u32[]{:S(2)}) copy-start(f32[4,8192]{1,0:T(4,128)} %weight_ref.1) | copy-start | bytes 393220
  5.5 13.1 %copy-start.1 = (s32[8192]{0:T(1024)S(1)}, s32[8192]{0:T(1024)}, u32[]{:S(2)}) copy-start(s32[8192]{0:T(1024)} %param.222) | copy-start | bytes 98308
  18.7 16.7 %collective-permute-start.6 = (f32[6,8,256]{2,1,0:T(8,128)S(1)}, f32[6,8,256]{2,1,0:T(8,128)S(1)}, u32[]{:S(2)}, u32[]{:S(2)}) collective-permute-start(f32[6,8,256]{2,1,0:T(8,128)S(1)} %get-tuple-element.639), channel_id=1, source_target_pairs={{0,64},{64,0},{1,65},{65,1},{2,66},{66,2},{3,67},{67,3},{4,68},{68... | collective-permute-start | bytes 147464 | tf_op jit(solution)/shard_map/cond/branch_1_fun/ppermute | solution.py:492
  21.4 13.9 %collective-permute-start.7 = (f32[6,8,256]{2,1,0:T(8,128)S(1)}, f32[6,8,256]{2,1,0:T(8,128)S(1)}, u32[]{:S(2)}, u32[]{:S(2)}) collective-permute-start(f32[6,8,256]{2,1,0:T(8,128)S(1)} %get-tuple-element.641), channel_id=1, source_target_pairs={{64,128},{128,64},{65,129},{129,65},{66,130},{130,66},{67,131},{13... | collective-permute-start | bytes 147464 | tf_op jit(solution)/shard_map/cond/branch_1_fun/ppermute | solution.py:493
  22.1 21.6 %collective-permute-start.5 = (f32[16,256]{1,0:T(8,128)S(1)}, f32[16,256]{1,0:T(8,128)S(1)}, u32[]{:S(2)}, u32[]{:S(2)}) collective-permute-start(f32[16,256]{1,0:T(8,128)S(1)} %get-tuple-element.635), channel_id=1, source_target_pairs={{192,480},{480,192},{193,481},{481,193},{194,482},{482,194},{195,4... | collective-permute-start | bytes 49160 | tf_op jit(solution)/shard_map/cond/branch_1_fun/ppermute | solution.py:497

commit v4 on v3

--- a/solution.py
+++ b/solution.py
@@ -91,10 +91,15 @@
     return 64 * (a // 4), EDGE * (a % 4)
 
 
+def rotate(x, shift):
+    shift %= 128
+    return pltpu.roll(x, shift, 1) if shift else x
+
+
 def pack_kernel(
     state_ref, damping_ref, axial_ref, angular_ref, shift_ref,
     first_ref, second_ref, held_ref, own_ref, matrices_ref,
-    which_ref, nearest_ref, exact_ref, back_ref, jac_ref, three_ref, sems,
+    which_ref, nearest_ref, move_ref, jac_ref, three_ref, sems,
 ):
     count = FIELDS + 1
     copies = []
@@ -104,7 +109,7 @@
     for n, ref in enumerate((axial_ref, angular_ref)):
         copies.append(pltpu.make_async_copy(ref, jac_ref.at[n], sems.at[count + n]))
     copies.append(pltpu.make_async_copy(shift_ref, three_ref, sems.at[count + 2]))
-    for copy in reversed(copies):
+    for copy in copies[count:] + copies[:count]:
         copy.start()
     even = lax.axis_index("sec") % 2 == 0
     lane = lanes((8, 128))
@@ -116,11 +121,14 @@
     at_last = jnp.where(s0 == last, 0, jnp.where(s1 == last, 1, 2))
     free = 3 - at_half - at_last
     shift = jnp.where(free == 0, s0, jnp.where(free == 1, s1, s2))
-    odd = shift & 1
+    odd = (shift & 1) == 1
     which_ref[0] = 2 * at_half + at_last - jnp.where(at_last > at_half, 1, 0)
-    nearest_ref[0] = jnp.where(shift >= last - 1, half - 1, lax.shift_right_logical(shift, 1))
-    exact_ref[0] = jnp.where(odd == 0, jnp.where(shift == last - 1, 0, 1), jnp.where(shift == last, 1, 0))
-    back_ref[0] = jnp.where(shift == last - 1, 1, 0)
+    by_last = (shift >= last - 1) | (shift == 0)
+    nearest = jnp.where(shift == 1, 0, lax.shift_right_logical(shift, 1) - 1)
+    nearest_ref[0] = jnp.where(by_last, half - 2, nearest)
+    less = (shift == last - 1) | (shift == 1)
+    forward = (shift == 0) | (odd & (shift != last))
+    move_ref[0] = jnp.where(less, 2, jnp.where(forward, 0, 1))
 
     scale = STEP * 2.0 / 3.0 * 0.5
     for n in range(2):
@@ -140,10 +148,10 @@
                 for k in range(4):
                     x = held_ref[a, pl.ds(8 * k + i, 8, stride=32), :]
                     place = 32 * k + spot(a)[1]
-                    here = (lane >= place) & (lane < place + EDGE)
-                    low = jnp.where(here, pltpu.roll(x, place, 1) if place else x, low)
-                    shift = (place + EDGE) % 128
-                    high = jnp.where(here, pltpu.roll(x, shift, 1) if shift else x, high)
+                    x = rotate(x, place)
+                    low = jnp.where((lane >= place) & (lane < place + EDGE), x, low)
+                    place = (place - EDGE) % 128
+                    high = jnp.where((lane >= place) & (lane < place + EDGE), x, high)
             rows = slice(64 * b + 8 * i, 64 * b + 8 * i + 8)
             own_ref[0, rows, :] = low
             own_ref[1, rows, :] = high
@@ -151,25 +159,19 @@
             second_ref[rows, :] = jnp.where(even, low, high)
         tops = jnp.zeros((8, 128), jnp.float32)
         for a in arrays:
-            top, place = held_ref[a, 248:256, :], 32 * (a % 4)
+            place = 32 * (a % 4)
+            top = rotate(held_ref[a, 248:256, :], place)
             wide = (lane >= place) & (lane < place + WIDE)
-            tops = jnp.where(wide, pltpu.roll(top, place, 1) if place else top, tops)
-            narrow = (lane >= place + WIDE) & (lane < place + 32)
-            shift = (place + 32) % 128
-            tops = jnp.where(narrow, pltpu.roll(top, shift, 1) if shift else top, tops)
+            place = (place - EDGE) % 128
+            tops = jnp.where(wide | ((lane >= place) & (lane < place + EDGE)), top, tops)
         first_ref[128 + 8 * b : 136 + 8 * b, :] = tops
         second_ref[128 + 8 * b : 136 + 8 * b, :] = tops
 
 
 def neighbours(even, first_ref, second_ref, rows):
     one = first_ref[jnp.where(even, 1, 0), rows, :]
-    two = second_ref[jnp.where(even, 0, 1), rows, :]
+    two = second_ref[rows, :]
     return jnp.where(even, one, two), jnp.where(even, two, one)
-
-
-def rotate(x, shift):
-    shift %= 128
-    return pltpu.roll(x, shift, 1) if shift else x
 
 
 def edge_kernel(
@@ -189,16 +191,16 @@
         right, left = neighbours(even, first_ref, second_ref, slice(128 + 8 * (a // 4), 136 + 8 * (a // 4)))
         top = 32 * (a % 4)
         high = jnp.concatenate(
-            [held_ref[a, 248:256, :], side(rotate(right, -top), rotate(left, 96 - top), WIDE)], axis=1
+            [held_ref[a, 248:256, :], side(rotate(right, -top), rotate(left, -top), WIDE)], axis=1
         )
         right, left = neighbours(even, first_ref, second_ref, pl.ds(start, 8, stride=8))
         low = jnp.concatenate(
-            [held_ref[a, 0:8, :], side(rotate(right, -place), rotate(left, -EDGE - place), EDGE)], axis=1
+            [held_ref[a, 0:8, :], side(rotate(right, -place), rotate(left, -place), EDGE)], axis=1
         )
         right, left = neighbours(even, first_ref, second_ref, pl.ds(start + 7, 8, stride=8))
         place = place + 64
         strip_ref[a, 0:8, 0:128] = held_ref[a, 240:248, :]
-        strip_ref[a, 0:8, 128:256] = side(rotate(right, -place), rotate(left, -EDGE - place), EDGE)
+        strip_ref[a, 0:8, 128:256] = side(rotate(right, -place), rotate(left, -place), EDGE)
         strip_ref[a, 8:16, :] = high
         rows_b_ref[a] = jnp.where(grp % 2 == 0, high, low)
         rows_c_ref[a] = jnp.where(grp == 2, low, high)
@@ -318,9 +320,9 @@
             rows = slice(start + 8 * i, start + 8 * i + 8)
             right, left = neighbours(even, first_ref, second_ref, rows)
             side[REACH + i] = choose(
-                rotate(left, -place),
+                rotate(left, 8 - place),
                 rotate(own_ref[0, rows, :], 8 - place),
-                rotate(own_ref[1, rows, :], 16 - place),
+                rotate(own_ref[1, rows, :], 24 - place),
                 rotate(right, 24 - place),
             )
         low, high = (
@@ -433,7 +435,14 @@
         [device(r, g, c), device(r, g, c + 1)] for r, g in everywhere for c in range(0, sectors, 2)
     ]
     chips = [
-        [device(r, g, c), device(r, g, c + 1)] for r, g in everywhere for c in range(1, sectors, 2)
+        pair
+        for r, g in everywhere
+        for c in range(1, sectors, 2)
+        for one, two in [(device(r, g, c), device(r, g, c + 1))]
+        for pair in ((one, two), (two, one))
+    ]
+    onward = [
+        (device(r, groups - 1, c + 1 - 2 * r), device(r, groups - 1, c)) for r in range(2) for c in range(sectors)
     ]
 
     def swap(lows):
@@ -465,20 +474,23 @@
             return lambda x: jnp.stack([lax.ppermute(x, AXES, opposite)] * 2)
         return lambda x: gather(x, across(shift))
 
-    branches = [branch(s) for s in range(0, sectors - 2, 2)] + [branch(sectors - 1)]
-
-    def moved(got, back):
+    branches = [branch(s) for s in range(2, sectors - 2, 2)] + [branch(sectors - 1)]
+
+    def mine(got):
+        return jnp.where(lax.axis_index("row") == 0, got[1], got[0])
+
+    def forth(got):
+        return jnp.stack([lax.ppermute(mine(got), AXES, onward)] * 2)
+
+    def back(got):
         row, even = lax.axis_index("row"), lax.axis_index("sec") % 2 == 0
-        mine = jnp.where(row == 0, got[1], got[0])
-        one, two = gather(mine, cores), gather(mine, chips)
-        ahead = jnp.where(even, one[1], two[1])
-        behind = jnp.where(even, two[0], one[0])
-        result = jnp.where((row == 0) != (back == 1), ahead, behind)
+        one, two = gather(mine(got), cores), lax.ppermute(mine(got), AXES, chips)
+        result = jnp.where(row == 0, jnp.where(even, two, one[0]), jnp.where(even, one[1], two))
         return jnp.stack([result, result])
 
-    def any_shift(send, nearest, exact, back):
+    def any_shift(send, nearest, move):
         got = lax.switch(nearest, branches, send)
-        return lax.switch(exact, [lambda got: moved(got, back), lambda got: got], got)
+        return lax.switch(move, [forth, lambda got: got, back], got)
 
     arrays = FIELDS + 1
     strip_shape = (FIELDS, 16, 256)
@@ -486,7 +498,7 @@
 
     def variant(at_half, at_last):
         def run(
-            nearest, exact, back, send,
+            nearest, move, send,
             strip, coeff, matrices, first, second, own, rows_b, rows_c, held,
         ):
             rows_b = lax.ppermute(rows_b, AXES, swap((0, 2)))
@@ -510,7 +522,7 @@
                 elif stage == at_last:
                     got = gather(send, across(sectors - 1))
                 else:
-                    got = any_shift(send, nearest, exact, back)
+                    got = any_shift(send, nearest, move)
                 if stage < 2:
                     strip_now, send = call(
                         functools.partial(strip_kernel, stage),
@@ -537,7 +549,7 @@
         first, second, held, own, matrices, *route = call(
             pack_kernel,
             [HBM] * 5,
-            [(144, 128)] * 2 + [(arrays, 256, 128), (2, 128, 128), (2 * ENTRIES, 8, 128)] + [ROUTE] * 4,
+            [(144, 128)] * 2 + [(arrays, 256, 128), (2, 128, 128), (2 * ENTRIES, 8, 128)] + [ROUTE] * 3,
             [
                 pltpu.VMEM((2, FIELDS, 1, FIELDS), jnp.float32),
                 pltpu.SMEM((3,), jnp.int32),
@@ -545,16 +557,16 @@
             ],
             vmem=58,
         )(state, damping, jnp.swapaxes(jac_axial, 0, 1), jnp.swapaxes(jac_angular, 0, 1), section_shift)
-        which, nearest, exact, back = (r.reshape(()) for r in route)
+        which, nearest, move = (r.reshape(()) for r in route)
+        second = lax.ppermute(second, AXES, chips)
         first = gather(first, cores)
-        second = gather(second, chips)
         rows_b, rows_c, send, strip, coeff = call(
             edge_kernel,
             [VMEM] * 5,
             [(arrays, 8, 256)] * 2 + [(16, 256), (arrays, 16, 256), (8, 256)],
         )(first, second, held, match_weight, donor_offset[None, :])
         return lax.switch(
-            which, variants, nearest, exact, back, send,
+            which, variants, nearest, move, send,
             strip, coeff, matrices, first, second, own, rows_b, rows_c, held,
         )
 

time: 67.7 us -> 63.6 us (0.939)
  blocking collectives: 36.8 us -> 22.7 us
  starting transfers between devices: 15.4 us -> 25.3 us
    all_gather x4 -> x3, blocking collectives: 36.8 us -> 22.7 us  [gather(): return lax.all_gather(x, AXES, axis_index_groups=members)]
    ppermute x0 -> x1, starting transfers between devices: none -> 12 us  [shards(): second = lax.ppermute(second, AXES, chips)]
    ppermute x1, starting transfers between devices: 12 us -> 9.89 us  [run(): got = lax.ppermute(send, AXES, opposite)]
  transfers between devices with their start and end apart: 3 -> 4, of which waited for: 0 -> 0; matrix products, arithmetic and copies ran while one was open for 0% -> 0% of each run, Pallas kernels for 12% -> 14%
where the time goes in v4:
time: 63.6 us; the launch traced here: 63.1 us
  starting transfers between devices  25.3 us (40%)
  blocking collectives  22.7 us (36%)
  Pallas kernels  12.1 us (19%)
  loops' own time  2.12 us (3%)
  between operations  0.89 us (1%)
    all_gather x3, blocking collectives, gather(): return lax.all_gather(x, AXES, axis_index_groups=members)  22.7 us
    ppermute x1, starting transfers between devices, shards(): second = lax.ppermute(second, AXES, chips)  12 us
    ppermute x1, starting transfers between devices, run(): got = lax.ppermute(send, AXES, opposite)  9.89 us
    pallas_call x1, Pallas kernels, run(): call(block_kernel, [VMEM] * 7, [(1, FIELDS, 256, 128)], [pltpu.VMEM(shape...  8.29 us
    ppermute x1, starting transfers between devices, run(): rows_b = lax.ppermute(rows_b, AXES, swap((0, 2)))  2.74 us
    pallas_call x1, Pallas kernels, shards(): call(pack_kernel, [HBM] * 5, [(144, 128)] * 2 + [(arrays, 256, 128), (2,...  2.42 us
    another operation x1, loops' own time, shards(): lax.switch(which, variants, nearest, move, send, strip, coeff, matrices,...  2.06 us
  transfers between devices with their start and end apart: 4, of which 0 were waited for; matrix products, arithmetic and copies ran while one was open for 0% of the time, Pallas kernels for 14%

profile of v4, /device:TPU:6, one launch (start us, length us, event | category | flops | bytes accessed | tf_op | source)
XLA Modules:
  0.0 63.1 jit_solution(1339383878290492374)
XLA Ops:
  0.0 2.4 %shard_map.79 = (f32[144,128]{1,0:T(8,128)}, f32[144,128]{1,0:T(8,128)}, f32[6,256,128]{2,1,0:T(8,128)S(1)}, f32[2,128,128]{2,1,0:T(8,128)S(1)}, f32[30,8,128]{2...) custom-call(f32[1,5,256,128]{3,2,1,0:T(8,128)} %state_ref.1, f32[1,256,128]{2,1,0:T(8,128)} %damping_ref.1, ...), custom_call_target="tpu_custom_call" | custom-call | tf_op jit(solution)/shard_map/pallas_call | solution.py:549
  2.4 0.0 copy-start
  2.4 12.0 %collective-permute-start.36 = (f32[144,128]{1,0:T(8,128)}, f32[144,128]{1,0:T(8,128)S(1)}, u32[]{:S(2)}, u32[]{:S(2)}) collective-permute-start(f32[144,128]{1,0:T(8,128)} %get-tuple-element.707), channel_id=1, source_target_pairs={{1,2},{2,1},{3,4},{4,3},{5,6},{6,5},{7,8},{8,7},{9,10},{10,9},{11,... | collective-permute-start | bytes 221192 | tf_op jit(solution)/shard_map/ppermute | solution.py:561
  15.1 0.0 copy-start.1
  15.1 2.1 %all-gather.186 = f32[288,128]{1,0:T(8,128)S(1)} all-gather(f32[144,128]{1,0:T(8,128)} %get-tuple-element.706), channel_id=188, replica_groups={{0,1},{2,3},{4,5},{6,7},{8,9},{10,11},{12,13},{14,15},{16,17},{18,19},{..., dimensions={0}, use_global_device_ids=true | all-gather | bytes 221184 | tf_op jit(solution)/shard_map/all_gather | solution.py:467
  17.2 0.0 collective-permute-done.36.second_ref
  17.2 0.0 copy-done
  17.2 0.0 copy-done.1
  17.2 0.1 shard_map.80
  17.3 45.6 %conditional.13 = (f32[1,5,256,128]{3,2,1,0:T(8,128)}) conditional(s32[]{:T(128)} %bitcast.230, (s32[]{:T(128)}, s32[]{:T(128)}, f32[16,256]{1,0:T(8,128)S(1)}, f32[6,8,256]{2,1,0:T(8,128)S(1)}, f32[6,8,256]{2,1,0:T(8,128)S(1)}, /*index=5*/f32[30,8,128]{2,1,0:T(8,128)S(1)}, f32[2,144,128]{2,1,0:T(8,128)S(1)}, ...), branch_computations={%region_0.35_spmd, %region_35.70_spmd, %region_70.105_spmd, %regio... | conditional | flops 40036884 | bytes 4950711 | solution.py:568
  17.5 2.7 %collective-permute-start.22 = (f32[6,8,256]{2,1,0:T(8,128)S(1)}, f32[6,8,256]{2,1,0:T(8,128)S(1)}, u32[]{:S(2)}, u32[]{:S(2)}) collective-permute-start(f32[6,8,256]{2,1,0:T(8,128)S(1)} %get-tuple-element.624), channel_id=1, source_target_pairs={{0,64},{64,0},{1,65},{65,1},{2,66},{66,2},{3,67},{67,3},{4,68},{68... | collective-permute-start | bytes 147464 | tf_op jit(solution)/shard_map/cond/branch_2_fun/ppermute | solution.py:504
  20.3 0.7 %collective-permute-start.23 = (f32[6,8,256]{2,1,0:T(8,128)S(1)}, f32[6,8,256]{2,1,0:T(8,128)S(1)}, u32[]{:S(2)}, u32[]{:S(2)}) collective-permute-start(f32[6,8,256]{2,1,0:T(8,128)S(1)} %get-tuple-element.626), channel_id=1, source_target_pairs={{64,128},{128,64},{65,129},{129,65},{66,130},{130,66},{67,131},{13... | collective-permute-start | bytes 147464 | tf_op jit(solution)/shard_map/cond/branch_2_fun/ppermute | solution.py:505
  21.0 7.2 %all-gather.92 = f32[32,256]{1,0:T(8,128)S(1)} all-gather(f32[16,256]{1,0:T(8,128)S(1)} %get-tuple-element.618), channel_id=94, replica_groups={{192,511},{193,448},{194,449},{195,450},{196,451},{197,452},{198,453},{..., dimensions={0}, use_global_device_ids=true | all-gather | bytes 49152 | tf_op jit(solution)/shard_map/cond/branch_2_fun/all_gather | solution.py:467
  28.1 0.2 branch_2_fun.4
  28.4 9.9 %collective-permute-start.21 = (f32[16,256]{1,0:T(8,128)S(1)}, f32[16,256]{1,0:T(8,128)S(1)}, u32[]{:S(2)}, u32[]{:S(2)}) collective-permute-start(f32[16,256]{1,0:T(8,128)S(1)} %get-tuple-element.620), channel_id=1, source_target_pairs={{192,480},{480,192},{193,481},{481,193},{194,482},{482,194},{195,4... | collective-permute-start | bytes 49160 | tf_op jit(solution)/shard_map/cond/branch_2_fun/ppermute | solution.py:509
  39.5 0.0 collective-permute-done.22.rows_b_ref
  39.5 0.0 collective-permute-done.23.rows_c_ref
  39.6 8.3 %branch_2_fun.5._ = f32[1,5,256,128]{3,2,1,0:T(8,128)} custom-call(f32[30,8,128]{2,1,0:T(8,128)S(1)} %get-tuple-element.614.matrices_ref, f32[2,144,128]{2,1,0:T(8,128)S(1)} %get-tuple-element.621.first_ref, f32[144,128]{1,0:T(8,128)S(1)} %get-tuple-element.622.second_ref, f32[2,128,128]{2,1,0:T(8,128)S(1)} %get-tuple-element.623.own_ref, ...), custom_call_target="tpu_custom_call" | custom-call | flops 40000000 | bytes 4000000 | tf_op jit(solution)/shard_map/cond/branch_2_fun/pallas_call | solution.py:514
  47.8 0.0 collective-permute-done.21.got_ref
  47.9 0.2 branch_2_fun.6
  48.1 13.5 %conditional.4 = (f32[2,16,256]{2,1,0:T(8,128)S(1)}) conditional(s32[]{:T(128)} %clamp.33, f32[16,256]{1,0:T(8,128)S(1)} %get-tuple-element.630, f32[16,256]{1,0:T(8,128)S(1)} %get-tuple-element.630, f32[16,256]{1,0:T(8,128)S(1)} %get-tuple-element.630, f32[16,256]{1,0:T(8,128)S(1)} %get-tuple-element.630, ...), branch_computations={%region_71.71_spmd, %region_72.72_spmd, %region_73.73_spmd, %regio... | conditional | flops 8192 | bytes 114736 | solution.py:492
  48.2 13.4 %all-gather.75 = f32[32,256]{1,0:T(8,128)S(1)} all-gather(f32[16,256]{1,0:T(8,128)S(1)} %param.83), channel_id=77, replica_groups={{192,476},{193,477},{194,478},{195,479},{196,480},{197,481},{198,482},{..., dimensions={0}, use_global_device_ids=true | all-gather | bytes 49152 | tf_op jit(solution)/shard_map/cond/branch_2_fun/cond/branch_13_fun/all_gather | solution.py:467
  61.6 0.8 %branch_2_fun.7 = f32[1,5,256,128]{3,2,1,0:T(8,128)} custom-call(f32[30,8,128]{2,1,0:T(8,128)S(1)} %get-tuple-element.614.matrices_ref, f32[8,256]{1,0:T(8,128)S(1)} %get-tuple-element.615.coeff_ref, f32[2,16,256]{2,1,0:T(8,128)S(1)} %get-tuple-element.728.got_ref, f32[6,16,256]{2,1,0:T(8,128)S(1)} %get-tuple-element.619.strip_ref, ...), custom_call_target="tpu_custom_call", output_to_operand_aliasing={{}: (5, {})} | custom-call | tf_op jit(solution)/shard_map/cond/branch_2_fun/pallas_call | solution.py:534
  (1 shorter events, 0.0 us)
Async XLA Ops:
  2.4 14.8 %copy-start = (f32[4,8192]{1,0:T(4,128)S(1)}, f32[4,8192]{1,0:T(4,128)}, u32[]{:S(2)}) copy-start(f32[4,8192]{1,0:T(4,128)} %weight_ref.1) | copy-start | bytes 393220
  2.4 14.8 %collective-permute-start.36 = (f32[144,128]{1,0:T(8,128)}, f32[144,128]{1,0:T(8,128)S(1)}, u32[]{:S(2)}, u32[]{:S(2)}) collective-permute-start(f32[144,128]{1,0:T(8,128)} %get-tuple-element.707), channel_id=1, source_target_pairs={{1,2},{2,1},{3,4},{4,3},{5,6},{6,5},{7,8},{8,7},{9,10},{10,9},{11,... | collective-permute-start | bytes 221192 | tf_op jit(solution)/shard_map/ppermute | solution.py:561
  15.1 2.1 %copy-start.1 = (s32[8192]{0:T(1024)S(1)}, s32[8192]{0:T(1024)}, u32[]{:S(2)}) copy-start(s32[8192]{0:T(1024)} %param.222) | copy-start | bytes 98308
  17.5 22.0 %collective-permute-start.22 = (f32[6,8,256]{2,1,0:T(8,128)S(1)}, f32[6,8,256]{2,1,0:T(8,128)S(1)}, u32[]{:S(2)}, u32[]{:S(2)}) collective-permute-start(f32[6,8,256]{2,1,0:T(8,128)S(1)} %get-tuple-element.624), channel_id=1, source_target_pairs={{0,64},{64,0},{1,65},{65,1},{2,66},{66,2},{3,67},{67,3},{4,68},{68... | collective-permute-start | bytes 147464 | tf_op jit(solution)/shard_map/cond/branch_2_fun/ppermute | solution.py:504
  20.3 19.3 %collective-permute-start.23 = (f32[6,8,256]{2,1,0:T(8,128)S(1)}, f32[6,8,256]{2,1,0:T(8,128)S(1)}, u32[]{:S(2)}, u32[]{:S(2)}) collective-permute-start(f32[6,8,256]{2,1,0:T(8,128)S(1)} %get-tuple-element.626), channel_id=1, source_target_pairs={{64,128},{128,64},{65,129},{129,65},{66,130},{130,66},{67,131},{13... | collective-permute-start | bytes 147464 | tf_op jit(solution)/shard_map/cond/branch_2_fun/ppermute | solution.py:505
  28.4 19.5 %collective-permute-start.21 = (f32[16,256]{1,0:T(8,128)S(1)}, f32[16,256]{1,0:T(8,128)S(1)}, u32[]{:S(2)}, u32[]{:S(2)}) collective-permute-start(f32[16,256]{1,0:T(8,128)S(1)} %get-tuple-element.620), channel_id=1, source_target_pairs={{192,480},{480,192},{193,481},{481,193},{194,482},{482,194},{195,4... | collective-permute-start | bytes 49160 | tf_op jit(solution)/shard_map/cond/branch_2_fun/ppermute | solution.py:509

commit v5 on v4

--- a/solution.py
+++ b/solution.py
@@ -17,7 +17,6 @@
 WIDE = 24
 SECTORS = 64
 ROUTE = (1,)
-UNROLL = 8
 REACH = 6
 
 VMEM = pl.BlockSpec(memory_space=pltpu.VMEM)
@@ -140,18 +139,19 @@
 
     for b in range(2):
         arrays = range(4 * b, min(4 * b + 4, count))
+        lows = [jnp.zeros((8, 128), jnp.float32)] * 8
+        highs = list(lows)
         for a in arrays:
             copies[a].wait()
-        for i in range(8):
-            low = high = jnp.zeros((8, 128), jnp.float32)
-            for a in arrays:
+            for i in range(8):
                 for k in range(4):
                     x = held_ref[a, pl.ds(8 * k + i, 8, stride=32), :]
                     place = 32 * k + spot(a)[1]
                     x = rotate(x, place)
-                    low = jnp.where((lane >= place) & (lane < place + EDGE), x, low)
+                    lows[i] = jnp.where((lane >= place) & (lane < place + EDGE), x, lows[i])
                     place = (place - EDGE) % 128
-                    high = jnp.where((lane >= place) & (lane < place + EDGE), x, high)
+                    highs[i] = jnp.where((lane >= place) & (lane < place + EDGE), x, highs[i])
+        for i, (low, high) in enumerate(zip(lows, highs)):
             rows = slice(64 * b + 8 * i, 64 * b + 8 * i + 8)
             own_ref[0, rows, :] = low
             own_ref[1, rows, :] = high
@@ -356,8 +356,8 @@
     def turns(x):
         return ([pltpu.roll(v, shift, 1) for v in x] for shift in (127, 1, 126, 2))
 
-    def near_stage(near, side_new, first, last, store):
-        @pl.loop(REACH + first, REACH + last, unroll=UNROLL)
+    def near_stage(near, side_new, first, last, unroll, store):
+        @pl.loop(REACH + first, REACH + last, unroll=unroll)
         def _(i):
             k = jnp.clip(lax.shift_right_arithmetic(i - REACH, 3), 0, 3)
             x, *others = axial(near, i)
@@ -399,16 +399,16 @@
         out_ref[0, f, pl.ds(i - REACH, 8, stride=32), :] = value
 
     side_stage(gx_ref, -4, 12, plain(gy_ref))
-    near_stage(x_ref, gy_ref, -4, 36, plain(y_ref))
+    near_stage(x_ref, gy_ref, -4, 36, 10, plain(y_ref))
     nothing_before(y_ref, gy_ref, 4)
     side_stage(gy_ref, -2, 10, plain(ge_ref))
-    near_stage(y_ref, ge_ref, -2, 34, blended(x_ref, (0.75, 0.25), into(z_ref)))
+    near_stage(y_ref, ge_ref, -2, 34, 9, blended(x_ref, (0.75, 0.25), into(z_ref)))
     for i in range(REACH - 2, REACH + 10):
         for f in fields:
             gz_ref[f, i] = 0.75 * gx_ref[f, i] + 0.25 * ge_ref[f, i]
     nothing_before(z_ref, gz_ref, 2)
     side_stage(gz_ref, 0, 8, plain(ge_ref))
-    near_stage(z_ref, ge_ref, 0, 32, blended(x_ref, (1.0 / 3.0, 2.0 / 3.0), out))
+    near_stage(z_ref, ge_ref, 0, 32, 8, blended(x_ref, (1.0 / 3.0, 2.0 / 3.0), out))
 
 
 def call(kernel, in_specs, out_shapes, scratch=(), out_specs=None, flops=0, vmem=40, **options):

time: 63.6 us -> 60 us (0.943)
  blocking collectives: 22.7 us -> 17.9 us
  starting transfers between devices: 25.3 us -> 26.5 us
    all_gather x3, blocking collectives: 22.7 us -> 17.9 us  [gather(): return lax.all_gather(x, AXES, axis_index_groups=members)]
    ppermute x1, starting transfers between devices: 9.89 us -> 11.1 us  [run(): got = lax.ppermute(send, AXES, opposite)]
where the time goes in v5:
time: 60 us; the launch traced here: 59.3 us
  starting transfers between devices  26.5 us (44%)
  blocking collectives  17.9 us (30%)
  Pallas kernels  12.1 us (20%)
  loops' own time  1.93 us (3%)
  between operations  0.89 us (1%)
    all_gather x3, blocking collectives, gather(): return lax.all_gather(x, AXES, axis_index_groups=members)  17.9 us
    ppermute x1, starting transfers between devices, shards(): second = lax.ppermute(second, AXES, chips)  12 us
    ppermute x1, starting transfers between devices, run(): got = lax.ppermute(send, AXES, opposite)  11.1 us
    pallas_call x1, Pallas kernels, run(): call(block_kernel, [VMEM] * 7, [(1, FIELDS, 256, 128)], [pltpu.VMEM(shape...  8.03 us
    ppermute x1, starting transfers between devices, run(): rows_b = lax.ppermute(rows_b, AXES, swap((0, 2)))  2.74 us
    pallas_call x1, Pallas kernels, shards(): call(pack_kernel, [HBM] * 5, [(144, 128)] * 2 + [(arrays, 256, 128), (2,...  2.69 us
    another operation x1, loops' own time, shards(): lax.switch(which, variants, nearest, move, send, strip, coeff, matrices,...  1.88 us
  transfers between devices with their start and end apart: 4, of which 0 were waited for; matrix products, arithmetic and copies ran while one was open for 0% of the time, Pallas kernels for 14%

profile of v5, /device:TPU:6, one launch (start us, length us, event | category | flops | bytes accessed | tf_op | source)
XLA Modules:
  0.0 59.3 jit_solution(3804888602143289387)
XLA Ops:
  0.0 2.7 %shard_map.79 = (f32[144,128]{1,0:T(8,128)}, f32[144,128]{1,0:T(8,128)}, f32[6,256,128]{2,1,0:T(8,128)S(1)}, f32[2,128,128]{2,1,0:T(8,128)S(1)}, f32[30,8,128]{2...) custom-call(f32[1,5,256,128]{3,2,1,0:T(8,128)} %state_ref.1, f32[1,256,128]{2,1,0:T(8,128)} %damping_ref.1, ...), custom_call_target="tpu_custom_call" | custom-call | tf_op jit(solution)/shard_map/pallas_call | solution.py:549
  2.7 0.0 copy-start
  2.7 12.0 %collective-permute-start.36 = (f32[144,128]{1,0:T(8,128)}, f32[144,128]{1,0:T(8,128)S(1)}, u32[]{:S(2)}, u32[]{:S(2)}) collective-permute-start(f32[144,128]{1,0:T(8,128)} %get-tuple-element.707), channel_id=1, source_target_pairs={{1,2},{2,1},{3,4},{4,3},{5,6},{6,5},{7,8},{8,7},{9,10},{10,9},{11,... | collective-permute-start | bytes 221192 | tf_op jit(solution)/shard_map/ppermute | solution.py:561
  15.3 0.0 copy-start.1
  15.3 2.1 %all-gather.186 = f32[288,128]{1,0:T(8,128)S(1)} all-gather(f32[144,128]{1,0:T(8,128)} %get-tuple-element.706), channel_id=188, replica_groups={{0,1},{2,3},{4,5},{6,7},{8,9},{10,11},{12,13},{14,15},{16,17},{18,19},{..., dimensions={0}, use_global_device_ids=true | all-gather | bytes 221184 | tf_op jit(solution)/shard_map/all_gather | solution.py:467
  17.5 0.0 collective-permute-done.36.second_ref
  17.5 0.0 copy-done
  17.5 0.0 copy-done.1
  17.5 0.1 shard_map.80
  17.6 41.5 %conditional.13 = (f32[1,5,256,128]{3,2,1,0:T(8,128)}) conditional(s32[]{:T(128)} %bitcast.230, (s32[]{:T(128)}, s32[]{:T(128)}, f32[16,256]{1,0:T(8,128)S(1)}, f32[6,8,256]{2,1,0:T(8,128)S(1)}, f32[6,8,256]{2,1,0:T(8,128)S(1)}, /*index=5*/f32[30,8,128]{2,1,0:T(8,128)S(1)}, f32[2,144,128]{2,1,0:T(8,128)S(1)}, ...), branch_computations={%region_0.35_spmd, %region_35.70_spmd, %region_70.105_spmd, %regio... | conditional | flops 40036884 | bytes 4950711 | solution.py:568
  17.9 2.7 %collective-permute-start.34 = (f32[6,8,256]{2,1,0:T(8,128)S(1)}, f32[6,8,256]{2,1,0:T(8,128)S(1)}, u32[]{:S(2)}, u32[]{:S(2)}) collective-permute-start(f32[6,8,256]{2,1,0:T(8,128)S(1)} %get-tuple-element.683), channel_id=1, source_target_pairs={{0,64},{64,0},{1,65},{65,1},{2,66},{66,2},{3,67},{67,3},{4,68},{68... | collective-permute-start | bytes 147464 | tf_op jit(solution)/shard_map/cond/branch_5_fun/ppermute | solution.py:504
  20.6 0.7 %collective-permute-start.35 = (f32[6,8,256]{2,1,0:T(8,128)S(1)}, f32[6,8,256]{2,1,0:T(8,128)S(1)}, u32[]{:S(2)}, u32[]{:S(2)}) collective-permute-start(f32[6,8,256]{2,1,0:T(8,128)S(1)} %get-tuple-element.685), channel_id=1, source_target_pairs={{64,128},{128,64},{65,129},{129,65},{66,130},{130,66},{67,131},{13... | collective-permute-start | bytes 147464 | tf_op jit(solution)/shard_map/cond/branch_5_fun/ppermute | solution.py:505
  22.5 8.7 %conditional.10 = (f32[2,16,256]{2,1,0:T(8,128)S(1)}) conditional(s32[]{:T(128)} %clamp.39, f32[16,256]{1,0:T(8,128)S(1)} %get-tuple-element.675, f32[16,256]{1,0:T(8,128)S(1)} %get-tuple-element.675, f32[16,256]{1,0:T(8,128)S(1)} %get-tuple-element.675, f32[16,256]{1,0:T(8,128)S(1)} %get-tuple-element.675, ...), branch_computations={%region_176.176_spmd, %region_177.177_spmd, %region_178.178_spmd, ... | conditional | flops 8192 | bytes 114736 | solution.py:492
  22.6 8.6 %all-gather.160 = f32[32,256]{1,0:T(8,128)S(1)} all-gather(f32[16,256]{1,0:T(8,128)S(1)} %param.180), channel_id=162, replica_groups={{192,460},{193,461},{194,462},{195,463},{196,464},{197,465},{198,466},{..., dimensions={0}, use_global_device_ids=true | all-gather | bytes 49152 | tf_op jit(solution)/shard_map/cond/branch_5_fun/cond/branch_5_fun/all_gather | solution.py:467
  31.2 0.2 branch_5_fun.4
  31.5 7.2 %all-gather.185 = f32[32,256]{1,0:T(8,128)S(1)} all-gather(f32[16,256]{1,0:T(8,128)S(1)} %get-tuple-element.677), channel_id=187, replica_groups={{192,511},{193,448},{194,449},{195,450},{196,451},{197,452},{198,453},{..., dimensions={0}, use_global_device_ids=true | all-gather | bytes 49152 | tf_op jit(solution)/shard_map/cond/branch_5_fun/all_gather | solution.py:467
  38.6 0.3 branch_5_fun.5
  38.9 11.1 %collective-permute-start.33 = (f32[16,256]{1,0:T(8,128)S(1)}, f32[16,256]{1,0:T(8,128)S(1)}, u32[]{:S(2)}, u32[]{:S(2)}) collective-permute-start(f32[16,256]{1,0:T(8,128)S(1)} %get-tuple-element.679), channel_id=1, source_target_pairs={{192,480},{480,192},{193,481},{481,193},{194,482},{482,194},{195,4... | collective-permute-start | bytes 49160 | tf_op jit(solution)/shard_map/cond/branch_5_fun/ppermute | solution.py:509
  50.0 0.0 collective-permute-done.34.rows_b_ref
  50.0 0.0 collective-permute-done.35.rows_c_ref
  50.0 8.0 %branch_5_fun.6._ = f32[1,5,256,128]{3,2,1,0:T(8,128)} custom-call(f32[30,8,128]{2,1,0:T(8,128)S(1)} %get-tuple-element.671.matrices_ref, f32[2,144,128]{2,1,0:T(8,128)S(1)} %get-tuple-element.680.first_ref, f32[144,128]{1,0:T(8,128)S(1)} %get-tuple-element.681.second_ref, f32[2,128,128]{2,1,0:T(8,128)S(1)} %get-tuple-element.682.own_ref, ...), custom_call_target="tpu_custom_call" | custom-call | flops 40000000 | bytes 4000000 | tf_op jit(solution)/shard_map/cond/branch_5_fun/pallas_call | solution.py:514
  58.0 0.0 collective-permute-done.33.got_ref
  58.0 0.8 %branch_5_fun.7 = f32[1,5,256,128]{3,2,1,0:T(8,128)} custom-call(f32[30,8,128]{2,1,0:T(8,128)S(1)} %get-tuple-element.671.matrices_ref, f32[8,256]{1,0:T(8,128)S(1)} %get-tuple-element.672.coeff_ref, f32[16,256]{1,0:T(8,128)S(1)} %collective-permute-done.33.got_ref, f32[6,16,256]{2,1,0:T(8,128)S(1)} %get-tuple-element.676.strip_ref, ...), custom_call_target="tpu_custom_call", output_to_operand_aliasing={{}: (5, {})} | custom-call | tf_op jit(solution)/shard_map/cond/branch_5_fun/pallas_call | solution.py:534
  (1 shorter events, 0.0 us)
Async XLA Ops:
  2.7 14.8 %copy-start = (f32[4,8192]{1,0:T(4,128)S(1)}, f32[4,8192]{1,0:T(4,128)}, u32[]{:S(2)}) copy-start(f32[4,8192]{1,0:T(4,128)} %weight_ref.1) | copy-start | bytes 393220
  2.7 14.8 %collective-permute-start.36 = (f32[144,128]{1,0:T(8,128)}, f32[144,128]{1,0:T(8,128)S(1)}, u32[]{:S(2)}, u32[]{:S(2)}) collective-permute-start(f32[144,128]{1,0:T(8,128)} %get-tuple-element.707), channel_id=1, source_target_pairs={{1,2},{2,1},{3,4},{4,3},{5,6},{6,5},{7,8},{8,7},{9,10},{10,9},{11,... | collective-permute-start | bytes 221192 | tf_op jit(solution)/shard_map/ppermute | solution.py:561
  15.3 2.1 %copy-start.1 = (s32[8192]{0:T(1024)S(1)}, s32[8192]{0:T(1024)}, u32[]{:S(2)}) copy-start(s32[8192]{0:T(1024)} %param.222) | copy-start | bytes 98308
  17.9 32.1 %collective-permute-start.34 = (f32[6,8,256]{2,1,0:T(8,128)S(1)}, f32[6,8,256]{2,1,0:T(8,128)S(1)}, u32[]{:S(2)}, u32[]{:S(2)}) collective-permute-start(f32[6,8,256]{2,1,0:T(8,128)S(1)} %get-tuple-element.683), channel_id=1, source_target_pairs={{0,64},{64,0},{1,65},{65,1},{2,66},{66,2},{3,67},{67,3},{4,68},{68... | collective-permute-start | bytes 147464 | tf_op jit(solution)/shard_map/cond/branch_5_fun/ppermute | solution.py:504
  20.6 29.4 %collective-permute-start.35 = (f32[6,8,256]{2,1,0:T(8,128)S(1)}, f32[6,8,256]{2,1,0:T(8,128)S(1)}, u32[]{:S(2)}, u32[]{:S(2)}) collective-permute-start(f32[6,8,256]{2,1,0:T(8,128)S(1)} %get-tuple-element.685), channel_id=1, source_target_pairs={{64,128},{128,64},{65,129},{129,65},{66,130},{130,66},{67,131},{13... | collective-permute-start | bytes 147464 | tf_op jit(solution)/shard_map/cond/branch_5_fun/ppermute | solution.py:505
  38.9 19.2 %collective-permute-start.33 = (f32[16,256]{1,0:T(8,128)S(1)}, f32[16,256]{1,0:T(8,128)S(1)}, u32[]{:S(2)}, u32[]{:S(2)}) collective-permute-start(f32[16,256]{1,0:T(8,128)S(1)} %get-tuple-element.679), channel_id=1, source_target_pairs={{192,480},{480,192},{193,481},{481,193},{194,482},{482,194},{195,4... | collective-permute-start | bytes 49160 | tf_op jit(solution)/shard_map/cond/branch_5_fun/ppermute | solution.py:509
